TPU v7x, 32 devices: a whole 2x2x4 slice. The times are simulated.
32 devices in a mesh: section: 2 (over core), fsdp: 4 (over y, x), tensor: 4 (over z).
Axes of the slice: x: 2, y: 2, z: 4, core: 2. Of those that a mesh axis runs over, the one named last changes fastest.
Arguments:
- hidden: bfloat16 [2, 512, 8192], P('section', 'fsdp', 'tensor'), may hold values from -16 to 16
- encoder_weight: bfloat16 [2, 1024, 8192], P('section', 'fsdp', 'tensor'), may hold values from -0.0625 to 0.0625
- decoder_weight: bfloat16 [2, 1024, 8192], P('section', 'fsdp', 'tensor'), may hold values from -16 to 16
- query_weight: bfloat16 [2, 8192, 8192], P('section', 'fsdp', 'tensor'), may hold values from -32 to 32
- key_weight: bfloat16 [2, 8192, 1024], P('section', 'fsdp', 'tensor'), may hold values from -1 to 1
- value_weight: bfloat16 [2, 8192, 1024], P('section', 'fsdp', 'tensor'), may hold values from -0.0625 to 0.0625
- segments: int32 [2, 4, 128], P('section', 'fsdp'), may hold values from 0 to 3, never falling along the last dimension, each value on 1 to 64 neighbouring positions
- out_grad: bfloat16 [2, 512, 8192], P('section', 'fsdp', 'tensor'), may hold values from -6 to 6
Outputs:
- attention: bfloat16 [2, 512, 8192], P('section', 'fsdp', 'tensor')
- hidden_grad: bfloat16 [2, 512, 8192], P('section', 'fsdp', 'tensor')
- encoder_grad: float32 [2, 1024, 8192], P('section', 'fsdp', 'tensor')
- decoder_grad: float32 [2, 1024, 8192], P('section', 'fsdp', 'tensor')
Inputs may be any that keep to these rules, and one draw needn't show every extreme that they name: `segments`: segment ids never fall along a row, and attention stays inside one document of one row; each document spans at most 64 tokens, and some document spans exactly that many.
All inputs are finite; a program needn't handle non-finite values.
Results may differ from a plain program's by a relative error of at most 0.025.
Values may be sent and summed in bfloat16 or wider, within the bound.
A program may use at most 128 MiB of HBM per device.

v0:
```python
import math

import jax
import jax.numpy as jnp
from jax import lax
from jax.sharding import PartitionSpec as P

D = 8192
DH = 128


NORM_EPS = 1e-05
ROPE_BASE = 500000.0
NEG_FILL = -1e30


def passed_along(value, axis, steps):
    count = lax.axis_size(axis)
    pairs = [(source, (source + steps) % count) for source in range(count)]
    return lax.ppermute(value, axis, pairs)


def rope_tables(segment_row, dim):
    length = segment_row.shape[0]
    positions = jnp.arange(length, dtype=jnp.int32)
    earlier = jnp.sum((segment_row[None, :] < segment_row[:, None]).astype(jnp.int32), axis=1)
    places = (positions - earlier).astype(jnp.float32)
    frequency = jnp.exp(jnp.arange(0, dim, 2).astype(jnp.float32) * (-math.log(ROPE_BASE) / dim))
    angles = places[:, None] * frequency[None, :]
    allowed = (segment_row[None, :] == segment_row[:, None]) & (
        positions[None, :] <= positions[:, None]
    )
    return (jnp.cos(angles), jnp.sin(angles), allowed)


def rotate(values, cosine, sine):
    half_dim = values.shape[-1] // 2
    first_half = values[..., :half_dim]
    second_half = values[..., half_dim:]
    cosine_rows = cosine[:, None, :]
    sine_rows = sine[:, None, :]
    return jnp.concatenate(
        [
            first_half * cosine_rows - second_half * sine_rows,
            second_half * cosine_rows + first_half * sine_rows,
        ],
        axis=-1,
    )


def unrotate(grads, cosine, sine):
    half_dim = grads.shape[-1] // 2
    first_half = grads[..., :half_dim]
    second_half = grads[..., half_dim:]
    cosine_rows = cosine[:, None, :]
    sine_rows = sine[:, None, :]
    return jnp.concatenate(
        [
            first_half * cosine_rows + second_half * sine_rows,
            second_half * cosine_rows - first_half * sine_rows,
        ],
        axis=-1,
    )


def product(form, left, right):
    return jnp.einsum(form, left, right, preferred_element_type=jnp.float32)


def attend(queries, keys_in, values_in, upstream, segment_row, head_count, pair_count):
    length = queries.shape[0]
    group_size = head_count // pair_count
    cosine, sine, allowed = rope_tables(segment_row, DH)
    query_rot = (
        rotate(queries.reshape(length, head_count, DH), cosine, sine)
        .astype(jnp.bfloat16)
        .reshape(length, pair_count, group_size, DH)
    )
    key_rot = rotate(keys_in.reshape(length, pair_count, DH), cosine, sine).astype(jnp.bfloat16)
    value_heads = values_in.reshape(length, pair_count, DH).astype(jnp.bfloat16)
    factor = 1.0 / math.sqrt(DH)
    scores = product("tkgd,skd->kgts", query_rot, key_rot) * factor
    scores = jnp.where(allowed, scores, NEG_FILL)
    row_max = jnp.max(scores, axis=-1, keepdims=True)
    exponent = jnp.exp(scores - row_max)
    probs = exponent / jnp.sum(exponent, axis=-1, keepdims=True)
    probs_low = probs.astype(jnp.bfloat16)
    mixed = product("kgts,skd->tkgd", probs_low, value_heads).reshape(length, head_count * DH)
    cot_heads = upstream.reshape(length, pair_count, group_size, DH)
    prob_grad = product("tkgd,skd->kgts", cot_heads, value_heads)
    value_grad = product("kgts,tkgd->skd", probs_low, cot_heads)
    score_grad = probs * (prob_grad - jnp.sum(probs * prob_grad, axis=-1, keepdims=True))
    score_grad_low = score_grad.astype(jnp.bfloat16)
    query_grad = product("kgts,skd->tkgd", score_grad_low, key_rot) * factor
    key_grad = product("kgts,tkgd->skd", score_grad_low, query_rot) * factor
    query_grad = unrotate(query_grad.reshape(length, head_count, DH), cosine, sine).reshape(
        length, head_count * DH
    )
    key_grad = unrotate(key_grad, cosine, sine).reshape(length, pair_count * DH)
    return (
        mixed.astype(jnp.bfloat16),
        query_grad.astype(jnp.bfloat16),
        key_grad.astype(jnp.bfloat16),
        value_grad.reshape(length, pair_count * DH).astype(jnp.bfloat16),
    )


def row_total(values):
    return lax.psum(values, "tensor")


def token_sum(left, right):
    return lax.psum_scatter(
        lax.dot_general(
            left, right, (((0,), (0,)), ((), ())), preferred_element_type=jnp.float32
        ).astype(jnp.bfloat16),
        "fsdp",
        scatter_dimension=0,
        tiled=True,
    ).astype(jnp.float32)


def body(
    hidden,
    encoder_weight,
    decoder_weight,
    query_weight,
    key_weight,
    value_weight,
    segments,
    out_grad,
):
    residual = hidden[0]
    segment_row = segments[0, 0]
    upstream = out_grad[0]
    contract_last = (((1,), (1,)), ((), ()))
    encoder_rows, decoder_rows = (
        lax.all_gather(encoder_weight[0], "fsdp", axis=0, tiled=True),
        lax.all_gather(decoder_weight[0], "fsdp", axis=0, tiled=True),
    )
    code_partial = lax.dot_general(
        residual, encoder_rows, contract_last, preferred_element_type=jnp.float32
    )
    code_sent = lax.psum(code_partial, "tensor").astype(jnp.bfloat16)
    code_received = passed_along(code_sent, "section", 1)
    decoded = jnp.dot(code_received, decoder_rows, preferred_element_type=jnp.float32)
    norm_factor = lax.rsqrt(row_total(jnp.sum(decoded * decoded, axis=1)) / D + NORM_EPS)[:, None]
    normed = (decoded * norm_factor).astype(jnp.bfloat16)
    normed_full = lax.all_gather(normed, "tensor", axis=1, tiled=True)
    query_width = query_weight.shape[2]
    key_width = key_weight.shape[2]
    joined = jnp.concatenate([query_weight[0], key_weight[0], value_weight[0]], axis=1)
    columns = lax.all_to_all(normed_full, "fsdp", split_axis=1, concat_axis=0, tiled=True)
    projected = lax.psum_scatter(
        jnp.dot(columns, joined, preferred_element_type=jnp.float32),
        "fsdp",
        scatter_dimension=0,
        tiled=True,
    )
    queries = projected[:, :query_width]
    keys_all = projected[:, query_width : query_width + key_width]
    values_all = projected[:, query_width + key_width :]
    mixed, query_grad, key_grad, value_grad = attend(
        queries, keys_all, values_all, upstream, segment_row, query_width // DH, key_width // DH
    )
    grad_joined = jnp.concatenate([query_grad, key_grad, value_grad], axis=1)
    grad_all = lax.all_gather(grad_joined, "fsdp", axis=0, tiled=True)
    partial_cols = lax.dot_general(
        grad_all, joined, contract_last, preferred_element_type=jnp.float32
    ).astype(jnp.bfloat16)
    back_full = lax.all_to_all(partial_cols, "fsdp", split_axis=0, concat_axis=1, tiled=True)
    normed_grad = lax.psum_scatter(
        back_full.astype(jnp.float32).astype(jnp.bfloat16),
        "tensor",
        scatter_dimension=1,
        tiled=True,
    ).astype(jnp.float32)
    inner_dot = row_total(jnp.sum(normed_grad * decoded, axis=1))[:, None]
    decoded_grad = (norm_factor * normed_grad - decoded * norm_factor**3 * inner_dot / D).astype(
        jnp.bfloat16
    )
    decoder_grad = token_sum(code_received, decoded_grad)
    code_grad_partial = lax.dot_general(
        decoded_grad, decoder_rows, contract_last, preferred_element_type=jnp.float32
    )
    code_grad_sent = lax.psum(code_grad_partial.astype(jnp.bfloat16), "tensor")
    code_grad = passed_along(code_grad_sent, "section", -1)
    encoder_grad = token_sum(code_grad, residual)
    hidden_grad = jnp.dot(code_grad, encoder_rows, preferred_element_type=jnp.float32).astype(
        jnp.bfloat16
    )
    return (mixed[None], hidden_grad[None], encoder_grad[None], decoder_grad[None])


def solution(mesh):
    placed = (
        P("section", "fsdp", "tensor"),
        P("section", "fsdp", "tensor"),
        P("section", "fsdp", "tensor"),
        P("section", "fsdp", "tensor"),
        P("section", "fsdp", "tensor"),
        P("section", "fsdp", "tensor"),
        P("section", "fsdp", None),
        P("section", "fsdp", "tensor"),
    )
    return jax.shard_map(
        body,
        mesh=mesh,
        in_specs=placed,
        out_specs=(
            P("section", "fsdp", "tensor"),
            P("section", "fsdp", "tensor"),
            P("section", "fsdp", "tensor"),
            P("section", "fsdp", "tensor"),
        ),
        check_vma=False,
    )
```

profile of v0, /device:TPU:0, one launch (start us, length us, event | category | flops | bytes accessed | tf_op | source)
XLA Modules:
  0.0 600.9 jit_solution(13161109661682517247)
XLA Ops:
  8.7 56.6 %all-gather.11.cloned.1.call-done = bf16[1,1024,2048]{2,1,0:T(8,128)(2,1)} async-done(((bf16[1,256,2048]{2,1,0:T(8,128)(2,1)}), bf16[1,1024,2048]{2,1,0:T(8,128)(2,1)}) %all-gather.11.cloned.1.call-update) | async-done | bytes 4194320 | tf_op jit(solution)/shard_map/all_gather | solution.py:138
  65.3 3.7 fusion.9
  69.0 30.4 %all-reduce.4 = bf16[128,1024]{1,0:T(8,128)(2,1)S(1)} all-reduce(f32[128,1024]{1,0:T(8,128)S(1)} %fusion.9), channel_id=1, replica_groups=mesh['section'=2,'fsdp'=4,'tensor'=4] {'tensor'}, use_global_device_ids=true, to_apply=%region_0.0 | all-reduce | flops 131072 | bytes 786432 | tf_op jit(solution)/shard_map/psum | solution.py:144
  99.5 20.3 %all-gather.13.cloned.1.call-done = bf16[1,1024,2048]{2,1,0:T(8,128)(2,1)} async-done(((bf16[1,256,2048]{2,1,0:T(8,128)(2,1)}), bf16[1,1024,2048]{2,1,0:T(8,128)(2,1)}) %all-gather.13.cloned.1.call-update) | async-done | bytes 4194320 | tf_op jit(solution)/shard_map/all_gather | solution.py:139
  119.9 3.0 multiply_reduce_fusion.1
  122.9 11.7 %psum.29 = f32[128]{0:T(128)S(1)} all-reduce(f32[128]{0:T(128)S(1)} %get-tuple-element.32), channel_id=1, replica_groups=mesh['section'=2,'fsdp'=4,'tensor'=4] {'tensor'}, use_global_device_ids=true, to_apply=%region_2.0 | all-reduce | flops 128 | bytes 1024 | tf_op jit(solution)/shard_map/psum | solution.py:109
  136.7 43.3 %all-gather.7.cloned.1.call-done = bf16[128,8192]{1,0:T(8,128)(2,1)} async-done(((bf16[128,2048]{1,0:T(8,128)(2,1)}), bf16[128,8192]{1,0:T(8,128)(2,1)}) %all-gather.7.cloned.1.call-update) | async-done | bytes 2097168 | tf_op jit(solution)/shard_map/all_gather | solution.py:149
  181.9 28.8 %all_to_all.38 = bf16[128,4,2048]{2,0,1:T(8,128)(2,1)S(1)} all-to-all(bf16[128,4,2048]{2,0,1:T(8,128)(2,1)S(1)} %bitcast.134), channel_id=1, replica_groups=mesh['section'=2,'fsdp'=4,'tensor'=4] {'fsdp'}, dimensions={1} | all-to-all | bytes 4194304 | tf_op jit(solution)/shard_map/all_to_all | solution.py:153
  210.6 10.2 %fusion.2 = f32[512,2560]{1,0:T(8,128)} fusion(bf16[512,2048]{1,0:T(8,128)(2,1)S(1)} %bitcast.139, bf16[2048,256]{1,0:T(8,128)(2,1)S(1)} %bitcast.162, bf16[2048,256]{1,0:T(8,128)(2,1)S(1)} %bitcast.164, bf16[2048,2048]{1,0:T(8,128)(2,1)} %bitcast.159), kind=kOutput, calls=%fused_computation.3 | convolution fusion | flops 5400166400 | bytes 17825792 | tf_op jit(solution)/shard_map/dot_general | solution.py:155
  222.7 57.3 %reduce-scatter.5.cloned.1.call-done = f32[128,2560]{1,0:T(8,128)} async-done(((f32[512,2560]{1,0:T(8,128)}), f32[128,2560]{1,0:T(8,128)}) %reduce-scatter.5.cloned.1.call-update) | async-done | bytes 1310736 | tf_op jit(solution)/shard_map/reduce_scatter | solution.py:154
  289.0 3.1 fusion.51
  308.6 39.7 %all-gather.9.cloned.1.call-done = bf16[512,2560]{1,0:T(8,128)(2,1)} async-done(((bf16[128,2560]{1,0:T(8,128)(2,1)}), bf16[512,2560]{1,0:T(8,128)(2,1)}) %all-gather.9.cloned.1.call-update) | async-done | bytes 2621456 | tf_op jit(solution)/shard_map/all_gather | solution.py:167
  348.3 9.2 %fusion.11 = bf16[512,2048]{1,0:T(8,128)(2,1)S(1)} fusion(bf16[512,2560]{1,0:T(8,128)(2,1)} %all-gather.9.cloned.1.call-done, bf16[2048,256]{1,0:T(8,128)(2,1)} %bitcast.161, bf16[2048,256]{1,0:T(8,128)(2,1)} %bitcast.163, bf16[2048,2048]{1,0:T(8,128)(2,1)} %bitcast.160), kind=kOutput, calls=%fused_computation.14 | convolution fusion | flops 5401214976 | bytes 15204352 | tf_op jit(solution)/shard_map/dot_general | solution.py:168
  357.5 28.1 %all_to_all.39 = bf16[4,128,2048]{2,1,0:T(8,128)(2,1)S(1)} all-to-all(bf16[4,128,2048]{2,1,0:T(8,128)(2,1)S(1)} %bitcast.140), channel_id=1, replica_groups=mesh['section'=2,'fsdp'=4,'tensor'=4] {'fsdp'}, dimensions={0} | all-to-all | bytes 4194304 | tf_op jit(solution)/shard_map/all_to_all | solution.py:171
  387.2 43.4 %reduce-scatter.7.cloned.1.call-done = bf16[128,2048]{1,0:T(8,128)(2,1)} async-done(((bf16[128,8192]{1,0:T(8,128)(2,1)}), bf16[128,2048]{1,0:T(8,128)(2,1)}) %reduce-scatter.7.cloned.1.call-update) | async-done | bytes 524304 | tf_op jit(solution)/shard_map/reduce_scatter | solution.py:172
  431.9 9.8 %psum.30 = f32[128]{0:T(128)S(1)} all-reduce(f32[128]{0:T(128)S(1)} %fusion.30), channel_id=1, replica_groups=mesh['section'=2,'fsdp'=4,'tensor'=4] {'tensor'}, use_global_device_ids=true, to_apply=%region_10.11 | all-reduce | flops 128 | bytes 1024 | tf_op jit(solution)/shard_map/psum | solution.py:109
  441.8 4.6 fusion.22
  446.4 3.4 convolution_convert_fusion
  450.2 30.0 %all-reduce.3.cloned.1.call-done = bf16[128,1024]{1,0:T(8,128)(2,1)} async-done(((bf16[128,1024]{1,0:T(8,128)(2,1)}), bf16[128,1024]{1,0:T(8,128)(2,1)}) %all-reduce.3.cloned.1.call-update) | async-done | bytes 262160 | tf_op jit(solution)/shard_map/psum | solution.py:186
  481.9 3.4 convolution_convert_fusion.1
  487.2 3.7 fusion.15
  491.0 44.6 %reduce-scatter.11.cloned.1.call-done = bf16[256,2048]{1,0:T(8,128)(2,1)} async-done(((bf16[1024,2048]{1,0:T(8,128)(2,1)}), bf16[256,2048]{1,0:T(8,128)(2,1)}) %reduce-scatter.11.cloned.1.call-update) | async-done | bytes 1048592 | tf_op jit(solution)/shard_map/reduce_scatter | solution.py:113
  535.6 2.8 bitcast_convert_fusion
  538.4 53.2 %reduce-scatter.9.cloned.1.call-done = bf16[256,2048]{1,0:T(8,128)(2,1)} async-done(((bf16[1024,2048]{1,0:T(8,128)(2,1)}), bf16[256,2048]{1,0:T(8,128)(2,1)}) %reduce-scatter.9.cloned.1.call-update) | async-done | bytes 1048592 | tf_op jit(solution)/shard_map/reduce_scatter | solution.py:113
  (106 shorter events, 42.4 us)
Async XLA Ops:
  7.2 58.1 %copy-start = (bf16[1,128,2048]{2,1,0:T(8,128)(2,1)S(1)}, bf16[1,128,2048]{2,1,0:T(8,128)(2,1)}, u32[]{:S(2)}) copy-start(bf16[1,128,2048]{2,1,0:T(8,128)(2,1)} %param.8) | copy-start | bytes 1572868
  7.2 58.1 %all-gather.11.cloned.1.call-start = ((), (), s32[]{:S(2)}) async-start(), calls=%async_computation.13 | async-start | bytes 5242880 | tf_op jit(solution)/shard_map/all_gather | solution.py:138
  7.9 112.0 %all-gather.13.cloned.1.call-start = ((), (), s32[]{:S(2)}) async-start(), calls=%async_computation.14 | async-start | bytes 5242880 | tf_op jit(solution)/shard_map/all_gather | solution.py:139
  8.7 171.3 %all-gather.7.cloned.1.call-start = ((), (), s32[]{:S(2)}) async-start(), calls=%async_computation.6 | async-start | bytes 2621440 | tf_op jit(solution)/shard_map/all_gather | solution.py:149
  99.5 20.4 %collective-permute-start = (bf16[128,1024]{1,0:T(8,128)(2,1)S(1)}, bf16[128,1024]{1,0:T(8,128)(2,1)S(1)}, u32[]{:S(2)}, u32[]{:S(2)}) collective-permute-start(bf16[128,1024]{1,0:T(8,128)(2,1)S(1)} %all-reduce.4), channel_id=1, source_target_pairs={{0,16},{16,0},{1,17},{17,1},{2,18},{18,2},{3,19},{19,3},{4,20},{20... | collective-permute-start | bytes 786440 | tf_op jit(solution)/shard_map/ppermute | solution.py:20
  136.7 143.3 %reduce-scatter.5.cloned.1.call-start = ((), (), s32[]{:S(2)}) async-start(), calls=%async_computation.7 | async-start | bytes 6553600 | tf_op jit(solution)/shard_map/reduce_scatter | solution.py:154
  180.0 30.6 %copy-start.19 = (bf16[1,2048,256]{2,1,0:T(8,128)(2,1)S(1)}, bf16[1,2048,256]{2,1,0:T(8,128)(2,1)}, u32[]{:S(2)}) copy-start(bf16[1,2048,256]{2,1,0:T(8,128)(2,1)} %param.13) | copy-start | bytes 3145732
  180.0 30.6 %copy-start.20 = (bf16[1,2048,256]{2,1,0:T(8,128)(2,1)S(1)}, bf16[1,2048,256]{2,1,0:T(8,128)(2,1)}, u32[]{:S(2)}) copy-start(bf16[1,2048,256]{2,1,0:T(8,128)(2,1)} %param.12) | copy-start | bytes 3145732
  220.8 127.5 %all-gather.9.cloned.1.call-start = ((), (), s32[]{:S(2)}) async-start(), calls=%async_computation.8 | async-start | bytes 3276800 | tf_op jit(solution)/shard_map/all_gather | solution.py:167
  222.1 69.9 %copy-start.7 = (bf16[1,128,2048]{1,2,0:T(8,128)(2,1)}, bf16[1,128,2048]{1,2,0:T(8,128)(2,1)S(1)}, u32[]{:S(2)}) copy-start(bf16[1,128,2048]{1,2,0:T(8,128)(2,1)S(1)} %copy.100) | copy-start | bytes 1572868
  284.2 9.5 %copy-start.2 = (bf16[128,16,64]{2,0,1:T(8,128)(2,1)}, bf16[128,16,64]{2,0,1:T(8,128)(2,1)S(1)}, u32[]{:S(2)}) copy-start(bf16[128,16,64]{2,0,1:T(8,128)(2,1)S(1)} %copy.59) | copy-start | bytes 786436
  308.6 122.0 %reduce-scatter.7.cloned.1.call-start = ((), (), s32[]{:S(2)}) async-start(), calls=%async_computation.9 | async-start | bytes 2621440 | tf_op jit(solution)/shard_map/reduce_scatter | solution.py:172
  385.6 56.1 %copy-start.16 = (f32[128]{0:T(128)S(1)}, f32[128]{0:T(128)}, u32[]{:S(2)}) copy-start(f32[128]{0:T(128)} %copy-done.15) | copy-start | bytes 1540
  385.6 56.1 %copy-start.18 = (f32[128]{0:T(128)S(1)}, f32[128]{0:T(128)}, u32[]{:S(2)}) copy-start(f32[128]{0:T(128)} %get-tuple-element.30) | copy-start | bytes 1540
  387.1 93.0 %all-reduce.3.cloned.1.call-start = ((), (), s32[]{:S(2)}) async-start(), calls=%async_computation.10 | async-start | bytes 524288 | tf_op jit(solution)/shard_map/psum | solution.py:186
  430.6 15.8 %copy-start.1 = (bf16[128,2048]{1,0:T(8,128)(2,1)S(1)}, bf16[128,2048]{1,0:T(8,128)(2,1)}, u32[]{:S(2)}) copy-start(bf16[128,2048]{1,0:T(8,128)(2,1)} %reduce-scatter.7.cloned.1.call-done) | copy-start | bytes 1572868
  446.4 89.2 %reduce-scatter.11.cloned.1.call-start = ((), (), s32[]{:S(2)}) async-start(), calls=%async_computation.12 | async-start | bytes 5242880 | tf_op jit(solution)/shard_map/reduce_scatter | solution.py:113
  449.8 35.5 %copy-start.3 = (bf16[128,16,64]{2,0,1:T(8,128)(2,1)S(1)}, bf16[128,16,64]{2,0,1:T(8,128)(2,1)}, u32[]{:S(2)}) copy-start(bf16[128,16,64]{2,0,1:T(8,128)(2,1)} %copy-done.2) | copy-start | bytes 786436
  449.8 35.5 %copy-start.9 = (bf16[128,2,64]{2,0,1:T(8,128)(2,1)S(1)}, bf16[128,2,64]{2,0,1:T(8,128)(2,1)}, u32[]{:S(2)}) copy-start(bf16[128,2,64]{2,0,1:T(8,128)(2,1)} %get-tuple-element.22) | copy-start | bytes 98308
  449.9 35.5 %copy-start.11 = (bf16[128,2,64]{2,0,1:T(8,128)(2,1)S(1)}, bf16[128,2,64]{2,0,1:T(8,128)(2,1)}, u32[]{:S(2)}) copy-start(bf16[128,2,64]{2,0,1:T(8,128)(2,1)} %get-tuple-element.23) | copy-start | bytes 98308
  449.9 35.5 %copy-start.12 = (bf16[128,2,128]{2,1,0:T(2,128)(2,1)S(1)}, bf16[128,2,128]{2,1,0:T(2,128)(2,1)}, u32[]{:S(2)}) copy-start(bf16[128,2,128]{2,1,0:T(2,128)(2,1)} %convert_element_type.96) | copy-start | bytes 196612
  449.9 35.5 %copy-start.14 = (f32[2,8,128]{2,1,0:T(8,128)S(1)}, f32[2,8,128]{2,1,0:T(8,128)}, u32[]{:S(2)}) copy-start(f32[2,8,128]{2,1,0:T(8,128)} %get-tuple-element.34) | copy-start | bytes 24580
  449.9 141.7 %reduce-scatter.9.cloned.1.call-start = ((), (), s32[]{:S(2)}) async-start(), calls=%async_computation.11 | async-start | bytes 5242880 | tf_op jit(solution)/shard_map/reduce_scatter | solution.py:113
  480.2 1.7 collective-permute-start.1
  (8 other events, 11.9 us)
Sparse Core Ops, SparseCore 0:
  9.9 55.3 all-gather.10
  67.1 52.6 all-gather.12
  136.8 43.1 all-gather.6
  221.0 58.9 reduce-scatter.4
  308.7 39.6 all-gather.8
  387.3 43.3 reduce-scatter.6
  446.5 33.6 all-reduce.2
  483.1 52.4 reduce-scatter.10
  538.8 52.6 reduce-scatter.8
where the time goes:
time: 602 us; the launch traced here: 601 us
  waiting for transfers between devices  392 us (65%)
  blocking collectives  109 us (18%)
  matrix products  52 us (9%)
  local copies, waits for them, and re-layouts  19.1 us (3%)
  other arithmetic  14.2 us (2%)
  between operations  14.2 us (2%)
    reduce_scatter x2, waiting for transfers between devices, token_sum(): lax.psum_scatter(lax.dot_general(left, right, (((0,), (0,)), ((), ())), p...  97.8 us
    reduce_scatter x1, waiting for transfers between devices, body(): lax.psum_scatter(jnp.dot(columns, joined, preferred_element_type=jnp.floa...  57.3 us
    all_gather x1, waiting for transfers between devices, body(): lax.all_gather(encoder_weight[0], 'fsdp', axis=0, tiled=True)  56.6 us
    reduce_scatter x1, waiting for transfers between devices, body(): lax.psum_scatter(back_full.astype(jnp.float32).astype(jnp.bfloat16), 'ten...  43.4 us
    all_gather x1, waiting for transfers between devices, body(): normed_full = lax.all_gather(normed, 'tensor', axis=1, tiled=True)  43.3 us
    all_gather x1, waiting for transfers between devices, body(): grad_all = lax.all_gather(grad_joined, 'fsdp', axis=0, tiled=True)  39.7 us
    psum x1, blocking collectives, body(): code_sent = lax.psum(code_partial, 'tensor').astype(jnp.bfloat16)  30.4 us
    psum x1, waiting for transfers between devices, body(): code_grad_sent = lax.psum(code_grad_partial.astype(jnp.bfloat16), 'tensor')  30 us
  transfers between devices with their start and end apart: 11, of which 10 were waited for; matrix products, arithmetic and copies ran while one was open for 3% of the time, Pallas kernels for 0%

commit v1 on v0

--- a/solution.py
+++ b/solution.py
@@ -1,8 +1,11 @@
+import functools
 import math
 
 import jax
 import jax.numpy as jnp
 from jax import lax
+from jax.experimental import pallas as pl
+from jax.experimental.pallas import tpu as pltpu
 from jax.sharding import PartitionSpec as P
 
 D = 8192
@@ -12,12 +15,6 @@
 NORM_EPS = 1e-05
 ROPE_BASE = 500000.0
 NEG_FILL = -1e30
-
-
-def passed_along(value, axis, steps):
-    count = lax.axis_size(axis)
-    pairs = [(source, (source + steps) % count) for source in range(count)]
-    return lax.ppermute(value, axis, pairs)
 
 
 def rope_tables(segment_row, dim):
@@ -105,19 +102,191 @@
     )
 
 
-def row_total(values):
-    return lax.psum(values, "tensor")
-
-
-def token_sum(left, right):
-    return lax.psum_scatter(
-        lax.dot_general(
-            left, right, (((0,), (0,)), ((), ())), preferred_element_type=jnp.float32
-        ).astype(jnp.bfloat16),
-        "fsdp",
-        scatter_dimension=0,
-        tiled=True,
-    ).astype(jnp.float32)
+MESH = pl.DeviceIdType.MESH
+
+
+def exchange_kernel(jobs, *refs):
+    count = len(jobs)
+    ins, outs, sems = refs[:count], refs[count : 2 * count], refs[2 * count :]
+    axes = []
+    for axis, _ in jobs:
+        if axis not in axes:
+            axes.append(axis)
+    barrier = pltpu.get_barrier_semaphore()
+    total = 0
+    for axis in axes:
+        size = lax.axis_size(axis)
+        me = lax.axis_index(axis)
+        for k in range(1, size):
+            peer = lax.rem(me + k, size)
+            pl.semaphore_signal(barrier, inc=1, device_id={axis: peer}, device_id_type=MESH)
+        total += size - 1
+    pl.semaphore_wait(barrier, total)
+    started = []
+    for index, (axis, mode) in enumerate(jobs):
+        send, recv, own = sems[3 * index : 3 * index + 3]
+        size = lax.axis_size(axis)
+        me = lax.axis_index(axis)
+        for k in range(1, size):
+            peer = lax.rem(me + k, size)
+            copy = pltpu.make_async_remote_copy(
+                src_ref=ins[index] if mode == "gather" else ins[index].at[peer],
+                dst_ref=outs[index].at[me],
+                send_sem=send.at[k],
+                recv_sem=recv.at[k],
+                device_id={axis: peer},
+                device_id_type=MESH,
+            )
+            copy.start()
+            started.append(copy)
+        local = pltpu.make_async_copy(
+            ins[index] if mode == "gather" else ins[index].at[me], outs[index].at[me], own
+        )
+        local.start()
+        started.append(local)
+    for copy in started:
+        copy.wait()
+
+
+def exchange(number, *work):
+    jobs = tuple((axis, mode) for _, axis, mode in work)
+    shapes, scratch = [], []
+    for value, axis, mode in work:
+        size = lax.axis_size(axis)
+        shape = (size,) + value.shape if mode == "gather" else value.shape
+        shapes.append(jax.ShapeDtypeStruct(shape, value.dtype))
+        scratch += [
+            pltpu.SemaphoreType.DMA((size,)),
+            pltpu.SemaphoreType.DMA((size,)),
+            pltpu.SemaphoreType.DMA,
+        ]
+    return pl.pallas_call(
+        functools.partial(exchange_kernel, jobs),
+        out_shape=shapes,
+        in_specs=[pl.BlockSpec(memory_space=pl.ANY)] * len(work),
+        out_specs=[pl.BlockSpec(memory_space=pl.ANY)] * len(work),
+        scratch_shapes=scratch,
+        compiler_params=pltpu.CompilerParams(collective_id=number, has_side_effects=True),
+    )(*[value for value, _, _ in work])
+
+
+def code_forward_kernel(chunk_ref, out_ref, send, recv):
+    sections, rows, cols = lax.axis_size("section"), lax.axis_size("fsdp"), lax.axis_size("tensor")
+    s, f, t = lax.axis_index("section"), lax.axis_index("fsdp"), lax.axis_index("tensor")
+    fold = cols // rows
+    after, before = lax.rem(s + 1, sections), lax.rem(s + sections - 1, sections)
+    barrier = pltpu.get_barrier_semaphore()
+    for r in range(rows):
+        for u in range(fold):
+            pl.semaphore_signal(
+                barrier, inc=1, device_id=(before, r, f * fold + u), device_id_type=MESH
+            )
+    pl.semaphore_wait(barrier, cols)
+    slot = f * fold + lax.rem(t, fold)
+    copies = []
+    for k in range(cols):
+        copy = pltpu.make_async_remote_copy(
+            src_ref=chunk_ref,
+            dst_ref=out_ref.at[slot],
+            send_sem=send.at[k],
+            recv_sem=recv.at[slot],
+            device_id=(after, t // fold, k),
+            device_id_type=MESH,
+        )
+        copy.start()
+        copies.append(copy)
+    for k in range(cols):
+        pltpu.make_async_remote_copy(
+            src_ref=chunk_ref,
+            dst_ref=out_ref.at[k],
+            send_sem=send.at[k],
+            recv_sem=recv.at[k],
+            device_id=(after, t // fold, k),
+            device_id_type=MESH,
+        ).wait_recv()
+    for copy in copies:
+        copy.wait_send()
+
+
+def code_forward(number, chunk):
+    cols = lax.axis_size("tensor")
+    return pl.pallas_call(
+        code_forward_kernel,
+        out_shape=jax.ShapeDtypeStruct((cols,) + chunk.shape, chunk.dtype),
+        in_specs=[pl.BlockSpec(memory_space=pl.ANY)],
+        out_specs=pl.BlockSpec(memory_space=pl.ANY),
+        scratch_shapes=[pltpu.SemaphoreType.DMA((cols,)), pltpu.SemaphoreType.DMA((cols,))],
+        compiler_params=pltpu.CompilerParams(collective_id=number, has_side_effects=True),
+    )(chunk)
+
+
+def code_back_kernel(chunk_ref, out_ref, send, recv):
+    sections, cols = lax.axis_size("section"), lax.axis_size("tensor")
+    s, f, t = lax.axis_index("section"), lax.axis_index("fsdp"), lax.axis_index("tensor")
+    after, before = lax.rem(s + 1, sections), lax.rem(s + sections - 1, sections)
+    barrier = pltpu.get_barrier_semaphore()
+    for k in range(cols):
+        pl.semaphore_signal(barrier, inc=1, device_id=(after, f, k), device_id_type=MESH)
+    pl.semaphore_wait(barrier, cols)
+    copies = []
+    for k in range(cols):
+        copy = pltpu.make_async_remote_copy(
+            src_ref=chunk_ref,
+            dst_ref=out_ref.at[t],
+            send_sem=send.at[k],
+            recv_sem=recv.at[t],
+            device_id=(before, f, k),
+            device_id_type=MESH,
+        )
+        copy.start()
+        copies.append(copy)
+    for k in range(cols):
+        pltpu.make_async_remote_copy(
+            src_ref=chunk_ref,
+            dst_ref=out_ref.at[k],
+            send_sem=send.at[k],
+            recv_sem=recv.at[k],
+            device_id=(before, f, k),
+            device_id_type=MESH,
+        ).wait_recv()
+    for copy in copies:
+        copy.wait_send()
+
+
+def code_back(number, chunk):
+    cols = lax.axis_size("tensor")
+    return pl.pallas_call(
+        code_back_kernel,
+        out_shape=jax.ShapeDtypeStruct((cols,) + chunk.shape, chunk.dtype),
+        in_specs=[pl.BlockSpec(memory_space=pl.ANY)],
+        out_specs=pl.BlockSpec(memory_space=pl.ANY),
+        scratch_shapes=[pltpu.SemaphoreType.DMA((cols,)), pltpu.SemaphoreType.DMA((cols,))],
+        compiler_params=pltpu.CompilerParams(collective_id=number, has_side_effects=True),
+    )(chunk)
+
+
+def dot_last(left, right):
+    return lax.dot_general(
+        left, right, (((1,), (1,)), ((), ())), preferred_element_type=jnp.float32
+    )
+
+
+def dot_first(left, right):
+    return lax.dot_general(
+        left, right, (((0,), (0,)), ((), ())), preferred_element_type=jnp.float32
+    )
+
+
+def dot(left, right):
+    return jnp.dot(left, right, preferred_element_type=jnp.float32)
+
+
+def summed(parts):
+    return jnp.sum(parts.astype(jnp.float32), axis=0)
+
+
+def as_rows(row):
+    return jnp.broadcast_to(row[None, :], (8, row.shape[0]))
 
 
 def body(
@@ -130,65 +299,97 @@
     segments,
     out_grad,
 ):
-    residual = hidden[0]
-    segment_row = segments[0, 0]
-    upstream = out_grad[0]
-    contract_last = (((1,), (1,)), ((), ()))
-    encoder_rows, decoder_rows = (
-        lax.all_gather(encoder_weight[0], "fsdp", axis=0, tiled=True),
-        lax.all_gather(decoder_weight[0], "fsdp", axis=0, tiled=True),
-    )
-    code_partial = lax.dot_general(
-        residual, encoder_rows, contract_last, preferred_element_type=jnp.float32
-    )
-    code_sent = lax.psum(code_partial, "tensor").astype(jnp.bfloat16)
-    code_received = passed_along(code_sent, "section", 1)
-    decoded = jnp.dot(code_received, decoder_rows, preferred_element_type=jnp.float32)
-    norm_factor = lax.rsqrt(row_total(jnp.sum(decoded * decoded, axis=1)) / D + NORM_EPS)[:, None]
-    normed = (decoded * norm_factor).astype(jnp.bfloat16)
-    normed_full = lax.all_gather(normed, "tensor", axis=1, tiled=True)
-    query_width = query_weight.shape[2]
-    key_width = key_weight.shape[2]
-    joined = jnp.concatenate([query_weight[0], key_weight[0], value_weight[0]], axis=1)
-    columns = lax.all_to_all(normed_full, "fsdp", split_axis=1, concat_axis=0, tiled=True)
-    projected = lax.psum_scatter(
-        jnp.dot(columns, joined, preferred_element_type=jnp.float32),
-        "fsdp",
-        scatter_dimension=0,
-        tiled=True,
-    )
-    queries = projected[:, :query_width]
-    keys_all = projected[:, query_width : query_width + key_width]
-    values_all = projected[:, query_width + key_width :]
+    low = jnp.bfloat16
+    rows, cols = lax.axis_size("fsdp"), lax.axis_size("tensor")
+    fold = cols // rows
+    residual, encoder, decoder = hidden[0], encoder_weight[0], decoder_weight[0]
+    wq, wk, wv = query_weight[0], key_weight[0], value_weight[0]
+    tokens, width = residual.shape
+    code_rows = encoder.shape[0]
+    query_width, key_width = wq.shape[1], wk.shape[1]
+
+    (hidden_all,) = exchange(0, (residual, "fsdp", "gather"))
+    decoder_rows = lax.all_gather(decoder, "fsdp", axis=0, tiled=True)
+    hidden_all = hidden_all.reshape(rows * tokens, width)
+    chunk = rows * tokens // cols
+    code_partial = dot_last(hidden_all, encoder).astype(low).reshape(cols, chunk, code_rows)
+    (code_parts,) = exchange(1, (code_partial, "tensor", "scatter"))
+    pieces = code_forward(2, summed(code_parts).astype(low))
+    code_received = (
+        pieces.reshape(rows, fold, chunk, code_rows)
+        .transpose(1, 2, 0, 3)
+        .reshape(tokens, rows * code_rows)
+    )
+    decoded = dot(code_received, decoder_rows)
+    square_sum = jnp.sum(decoded * decoded, axis=1)
+    decoded_all, square_all, encoder_rows = exchange(
+        3,
+        (decoded.astype(low), "tensor", "gather"),
+        (as_rows(square_sum), "tensor", "gather"),
+        (encoder, "fsdp", "gather"),
+    )
+    encoder_rows = encoder_rows.reshape(rows * code_rows, width)
+    norm_factor = lax.rsqrt(jnp.sum(square_all[:, 0], axis=0) / D + NORM_EPS)[:, None]
+    (columns,) = exchange(
+        4, (decoded_all.reshape(rows, fold, tokens, width), "fsdp", "scatter")
+    )
+    columns = columns.transpose(0, 2, 1, 3).reshape(rows * tokens, fold * width)
+    query_parts, key_parts, value_parts = exchange(
+        5,
+        (dot(columns, wq).astype(low).reshape(rows, tokens, query_width), "fsdp", "scatter"),
+        (dot(columns, wk).astype(low).reshape(rows, tokens, key_width), "fsdp", "scatter"),
+        (dot(columns, wv).astype(low).reshape(rows, tokens, key_width), "fsdp", "scatter"),
+    )
     mixed, query_grad, key_grad, value_grad = attend(
-        queries, keys_all, values_all, upstream, segment_row, query_width // DH, key_width // DH
-    )
-    grad_joined = jnp.concatenate([query_grad, key_grad, value_grad], axis=1)
-    grad_all = lax.all_gather(grad_joined, "fsdp", axis=0, tiled=True)
-    partial_cols = lax.dot_general(
-        grad_all, joined, contract_last, preferred_element_type=jnp.float32
-    ).astype(jnp.bfloat16)
-    back_full = lax.all_to_all(partial_cols, "fsdp", split_axis=0, concat_axis=1, tiled=True)
-    normed_grad = lax.psum_scatter(
-        back_full.astype(jnp.float32).astype(jnp.bfloat16),
-        "tensor",
-        scatter_dimension=1,
-        tiled=True,
-    ).astype(jnp.float32)
-    inner_dot = row_total(jnp.sum(normed_grad * decoded, axis=1))[:, None]
+        summed(query_parts) * norm_factor,
+        summed(key_parts) * norm_factor,
+        summed(value_parts) * norm_factor,
+        out_grad[0],
+        segments[0, 0],
+        query_width // DH,
+        key_width // DH,
+    )
+    code_split = code_received.reshape(tokens, rows, code_rows).transpose(1, 0, 2)
+    query_grads, key_grads, value_grads, code_all = exchange(
+        6,
+        (query_grad, "fsdp", "gather"),
+        (key_grad, "fsdp", "gather"),
+        (value_grad, "fsdp", "gather"),
+        (code_split, "fsdp", "scatter"),
+    )
+    whole = rows * tokens
+    partial_cols = (
+        dot_last(query_grads.reshape(whole, query_width), wq)
+        + dot_last(key_grads.reshape(whole, key_width), wk)
+        + dot_last(value_grads.reshape(whole, key_width), wv)
+    ).astype(low)
+    (back,) = exchange(7, (partial_cols.reshape(rows, tokens, fold * width), "fsdp", "scatter"))
+    back = back.reshape(rows, tokens, fold, width).transpose(0, 2, 1, 3)
+    (grad_parts,) = exchange(8, (back.reshape(cols, tokens, width), "tensor", "scatter"))
+    normed_grad = summed(grad_parts)
+    (inner_parts,) = exchange(
+        9, (as_rows(jnp.sum(normed_grad * decoded, axis=1)), "tensor", "gather")
+    )
+    inner_dot = jnp.sum(inner_parts[:, 0], axis=0)[:, None]
     decoded_grad = (norm_factor * normed_grad - decoded * norm_factor**3 * inner_dot / D).astype(
-        jnp.bfloat16
-    )
-    decoder_grad = token_sum(code_received, decoded_grad)
-    code_grad_partial = lax.dot_general(
-        decoded_grad, decoder_rows, contract_last, preferred_element_type=jnp.float32
-    )
-    code_grad_sent = lax.psum(code_grad_partial.astype(jnp.bfloat16), "tensor")
-    code_grad = passed_along(code_grad_sent, "section", -1)
-    encoder_grad = token_sum(code_grad, residual)
-    hidden_grad = jnp.dot(code_grad, encoder_rows, preferred_element_type=jnp.float32).astype(
-        jnp.bfloat16
-    )
+        low
+    )
+    grad_partial = dot_last(decoded_grad, decoder_rows).astype(low)
+    code_grad_parts, decoded_grads = exchange(
+        10,
+        (grad_partial.reshape(cols, tokens // cols, rows * code_rows), "tensor", "scatter"),
+        (decoded_grad, "fsdp", "gather"),
+    )
+    code_grad = code_back(11, summed(code_grad_parts).astype(low))
+    code_grad = code_grad.reshape(tokens, rows * code_rows)
+    (code_grads,) = exchange(
+        12, (code_grad.reshape(tokens, rows, code_rows).transpose(1, 0, 2), "fsdp", "scatter")
+    )
+    hidden_grad = dot(code_grad, encoder_rows).astype(low)
+    decoder_grad = dot_first(
+        code_all.reshape(whole, code_rows), decoded_grads.reshape(whole, width)
+    )
+    encoder_grad = dot_first(code_grads.reshape(whole, code_rows), hidden_all)
     return (mixed[None], hidden_grad[None], encoder_grad[None], decoder_grad[None])
 
 

time: 602 us -> 427 us (0.71)
  waiting for transfers between devices: 392 us -> 8.49 us
  Pallas kernels: 0 us -> 318 us
  blocking collectives: 109 us -> 0 us
    pallas_call x0 -> x13, Pallas kernels: none -> 318 us  [the longest x11 300 us: exchange(): pl.pallas_call(functools.partial(exchange_kernel, jobs), out_shape=shapes...]
    reduce_scatter x4 -> x0, waiting for transfers between devices: 199 us -> none  [the longest x2 97.8 us: token_sum(): lax.psum_scatter(lax.dot_general(left, right, (((0,), (0,)), ((), ())), p...]
    all_gather x4 -> x1, waiting for transfers between devices: 160 us -> 7.81 us  [body(): decoder_rows = lax.all_gather(decoder, 'fsdp', axis=0, tiled=True)]
    all_to_all x2 -> x0, blocking collectives: 56.9 us -> none  [the longest x1 28.8 us: body(): lax.all_to_all(normed_full, 'fsdp', split_axis=1, concat_axis=0, tiled=True)]
    psum x3 -> x0, blocking collectives: 52 us -> none  [the longest x1 30.4 us: body(): code_sent = lax.psum(code_partial, 'tensor').astype(jnp.bfloat16)]
    psum x1 -> x0, waiting for transfers between devices: 30 us -> none  [body(): code_grad_sent = lax.psum(code_grad_partial.astype(jnp.bfloat16), 'tensor')]
    reduce_sum x1 -> x8, other arithmetic: 1.3 us -> 10.4 us  [the longest x5 8.57 us: summed(): return jnp.sum(parts.astype(jnp.float32), axis=0)]
    dot_general x8 -> x12, matrix products: 41.1 us -> 42.5 us  [the longest x5 18.8 us: dot(): return jnp.dot(left, right, preferred_element_type=jnp.float32)]
  transfers between devices with their start and end apart: 11 -> 1, of which waited for: 10 -> 1; matrix products, arithmetic and copies ran while one was open for 3% -> 2% of each run, Pallas kernels for 0% -> 14%
where the time goes in v1:
time: 427 us
  Pallas kernels  318 us (74%)
  matrix products  52.2 us (12%)
  local copies, waits for them, and re-layouts  17.3 us (4%)
  other arithmetic  15.5 us (4%)
  between operations  14.5 us (3%)
  waiting for transfers between devices  8.49 us (2%)
    pallas_call x11, Pallas kernels, exchange(): pl.pallas_call(functools.partial(exchange_kernel, jobs), out_shape=shapes...  300 us
    dot_general x5, matrix products, dot(): return jnp.dot(left, right, preferred_element_type=jnp.float32)  18.8 us
    dot_general x5, matrix products, dot_last(): lax.dot_general(left, right, (((1,), (1,)), ((), ())), preferred_element_...  18.5 us
    pallas_call x1, Pallas kernels, code_forward(): pl.pallas_call(code_forward_kernel, out_shape=jax.ShapeDtypeStruct((cols,...  10 us
    reduce_sum x5, other arithmetic, summed(): return jnp.sum(parts.astype(jnp.float32), axis=0)  8.57 us
  transfers between devices with their start and end apart: 1, of which 1 were waited for; matrix products, arithmetic and copies ran while one was open for 2% of the time, Pallas kernels for 14%

profile of v1, /device:TPU:0, one launch (start us, length us, event | category | flops | bytes accessed | tf_op | source)
XLA Modules:
  0.0 426.5 jit_solution(1811846916536480361)
XLA Ops:
  10.1 39.0 %shard_map.111 = bf16[4,128,2048]{2,1,0:T(8,128)(2,1)} custom-call(bf16[128,2048]{1,0:T(8,128)(2,1)} %bitcast.196), custom_call_target="tpu_custom_call" | custom-call | tf_op jit(solution)/shard_map/pallas_call | solution.py:163
  49.1 3.0 convolution_convert_fusion.4
  52.1 9.1 %shard_map.112 = bf16[4,128,256]{2,1,0:T(8,128)(2,1)} custom-call(bf16[4,128,256]{2,1,0:T(8,128)(2,1)} %bitcast.205), custom_call_target="tpu_custom_call" | custom-call | tf_op jit(solution)/shard_map/pallas_call | solution.py:163
  62.9 10.0 %shard_map.113.refs_3_ = bf16[4,128,256]{2,1,0:T(8,128)(2,1)} custom-call(bf16[128,256]{1,0:T(8,128)(2,1)} %reduce_sum.129.chunk_ref), custom_call_target="tpu_custom_call" | custom-call | tf_op jit(solution)/shard_map/pallas_call | solution.py:213
  74.5 7.8 %all-gather.3.cloned.1.call-done = bf16[1,1024,2048]{2,1,0:T(8,128)(2,1)} async-done(((bf16[1,256,2048]{2,1,0:T(8,128)(2,1)}), bf16[1,1024,2048]{2,1,0:T(8,128)(2,1)}) %all-gather.3.cloned.1.call-update) | async-done | bytes 4194320 | tf_op jit(solution)/shard_map/all_gather | solution.py:312
  82.4 3.7 multiply_reduce_fusion.2
  86.7 52.4 %shard_map.114 = (bf16[4,128,2048]{2,1,0:T(8,128)(2,1)}, f32[4,8,128]{2,1,0:T(8,128)}, bf16[4,256,2048]{2,1,0:T(8,128)(2,1)}) custom-call(bf16[128,2048]{1,0:T(8,128)(2,1)} %get-tuple-element.47.refs_0_, f32[8,128]{1,0:T(8,128)} %broadcast_in_dim.18.refs_1_, bf16[256,2048]{1,0:T(8,128)(2,1)} %bitcast.194), custom_call_target="tpu_custom_call" | custom-call | tf_op jit(solution)/shard_map/pallas_call | solution.py:163
  139.1 26.0 %shard_map.115 = bf16[4,1,128,2048]{3,2,1,0:T(8,128)(2,1)} custom-call(bf16[4,1,128,2048]{3,2,1,0:T(8,128)(2,1)} %bitcast.183), custom_call_target="tpu_custom_call" | custom-call | tf_op jit(solution)/shard_map/pallas_call | solution.py:163
  166.6 3.0 convolution_convert_fusion.2
  171.1 9.1 %fusion.9 = bf16[512,2048]{1,0:T(8,128)(2,1)} fusion(bf16[512,2048]{1,0:T(8,128)(2,1)S(1)} %bitcast.182, bf16[1,2048,2048]{2,1,0:T(8,128)(2,1)} %param.11), kind=kOutput, calls=%fused_computation.12 | convolution fusion | flops 4296015872 | bytes 12582912 | tf_op jit(solution)/shard_map/dot_general | solution.py:281
  180.2 31.4 %shard_map.116 = (bf16[4,128,2048]{2,1,0:T(8,128)(2,1)}, bf16[4,128,256]{2,1,0:T(8,128)(2,1)}, bf16[4,128,256]{2,1,0:T(8,128)(2,1)}) custom-call(bf16[4,128,2048]{2,1,0:T(8,128)(2,1)} %bitcast.177, bf16[4,128,256]{2,1,0:T(8,128)(2,1)} %bitcast.204, bf16[4,128,256]{2,1,0:T(8,128)(2,1)} %bitcast.203), custom_call_target="tpu_custom_call" | custom-call | tf_op jit(solution)/shard_map/pallas_call | solution.py:163
  218.9 2.5 fusion.22
  221.4 2.4 convolution_convert_fusion.1
  233.0 2.4 copy.98
  238.9 34.0 %shard_map.117 = (bf16[4,128,2048]{2,1,0:T(8,128)(2,1)}, bf16[4,128,256]{2,1,0:T(8,128)(2,1)}, bf16[4,128,256]{2,1,0:T(8,128)(2,1)}, bf16[4,128,256]{2,1,0:T(8,128)(2,1)}) custom-call(bf16[128,2048]{1,0:T(8,128)(2,1)} %bitcast.179, bf16[128,256]{1,0:T(8,128)(2,1)} %copy_bitcast_fusion.2.refs_1_, bf16[128,256]{1,0:T(8,128)(2,1)} %copy.97.refs_2_, ...), custom_call_target="tpu_custom_call" | custom-call | tf_op jit(solution)/shard_map/pallas_call | solution.py:163
  272.9 7.9 %fusion.1 = f32[512,2048]{1,0:T(8,128)S(1)} fusion(bf16[512,2048]{1,0:T(8,128)(2,1)} %bitcast.210, bf16[1,2048,2048]{2,1,0:T(8,128)(2,1)} %param.11), kind=kOutput, calls=%fused_computation.1 | convolution fusion | flops 4294967296 | bytes 14680064 | tf_op jit(solution)/shard_map/dot_general | solution.py:269
  284.3 23.8 %shard_map.118.refs_0_ = bf16[4,128,2048]{2,1,0:T(8,128)(2,1)} custom-call(bf16[4,128,2048]{2,1,0:T(8,128)(2,1)} %bitcast.171), custom_call_target="tpu_custom_call" | custom-call | tf_op jit(solution)/shard_map/pallas_call | solution.py:163
  308.1 37.8 %shard_map.119 = bf16[4,128,2048]{2,1,0:T(8,128)(2,1)} custom-call(bf16[4,128,2048]{2,1,0:T(8,128)(2,1)} %shard_map.118.refs_0_), custom_call_target="tpu_custom_call" | custom-call | tf_op jit(solution)/shard_map/pallas_call | solution.py:163
  348.7 15.1 %shard_map.120 = f32[4,8,128]{2,1,0:T(8,128)} custom-call(f32[8,128]{1,0:T(8,128)} %broadcast_in_dim.21.refs_0_), custom_call_target="tpu_custom_call" | custom-call | tf_op jit(solution)/shard_map/pallas_call | solution.py:163
  364.8 4.6 %fusion.17 = bf16[128,1024]{1,0:T(8,128)(2,1)} fusion(bf16[128,2048]{1,0:T(8,128)(2,1)S(1)} %subtract_convert_fusion.refs_1_, bf16[1,1024,2048]{2,1,0:T(8,128)(2,1)} %all-gather.3.cloned.1.call-done), kind=kOutput, calls=%fused_computation.28 | convolution fusion | flops 537001984 | bytes 4980736 | tf_op jit(solution)/shard_map/dot_general | solution.py:269
  369.5 25.3 %shard_map.121 = (bf16[4,32,1024]{2,1,0:T(8,128)(2,1)}, bf16[4,128,2048]{2,1,0:T(8,128)(2,1)}) custom-call(bf16[4,32,1024]{2,1,0:T(8,128)(2,1)} %bitcast.192, bf16[128,2048]{1,0:T(8,128)(2,1)} %copy-done.2), custom_call_target="tpu_custom_call" | custom-call | tf_op jit(solution)/shard_map/pallas_call | solution.py:163
  396.4 8.4 %shard_map.122 = bf16[4,32,1024]{2,1,0:T(8,128)(2,1)} custom-call(bf16[32,1024]{1,0:T(8,128)(2,1)} %reduce_sum.144.chunk_ref), custom_call_target="tpu_custom_call" | custom-call | tf_op jit(solution)/shard_map/pallas_call | solution.py:258
  406.7 6.1 %shard_map.123 = bf16[4,128,256]{2,1,0:T(8,128)(2,1)} custom-call(bf16[4,128,256]{2,1,0:T(8,128)(2,1)} %bitcast.195), custom_call_target="tpu_custom_call" | custom-call | tf_op jit(solution)/shard_map/pallas_call | solution.py:163
  412.9 3.1 convolution_bitcast_fusion.1
  (91 shorter events, 43.9 us)
Async XLA Ops:
  7.2 162.5 %copy-start = (bf16[1,2048,256]{2,1,0:T(8,128)(2,1)S(1)}, bf16[1,2048,256]{2,1,0:T(8,128)(2,1)}, u32[]{:S(2)}) copy-start(bf16[1,2048,256]{2,1,0:T(8,128)(2,1)} %param.12) | copy-start | bytes 3145732
  7.2 75.2 %all-gather.3.cloned.1.call-start = ((), (), s32[]{:S(2)}) async-start(), calls=%async_computation | async-start | bytes 5242880 | tf_op jit(solution)/shard_map/all_gather | solution.py:312
  7.9 41.2 %copy-start.9 = (bf16[1,256,2048]{2,1,0:T(8,128)(2,1)S(1)}, bf16[1,256,2048]{2,1,0:T(8,128)(2,1)}, u32[]{:S(2)}) copy-start(bf16[1,256,2048]{2,1,0:T(8,128)(2,1)} %param.9) | copy-start | bytes 3145732
  49.1 24.9 %copy-start.17 = (s32[1,1,128]{2,1,0:T(1,128)S(1)}, s32[1,1,128]{2,1,0:T(1,128)}, u32[]{:S(2)}) copy-start(s32[1,1,128]{2,1,0:T(1,128)} %param.14) | copy-start | bytes 1540
  139.1 27.5 %copy-start.7 = (bf16[1,2048,256]{2,1,0:T(8,128)(2,1)S(1)}, bf16[1,2048,256]{2,1,0:T(8,128)(2,1)}, u32[]{:S(2)}) copy-start(bf16[1,2048,256]{2,1,0:T(8,128)(2,1)} %param.13) | copy-start | bytes 3145732
  165.2 4.5 %copy-start.6 = (bf16[4,1,128,2048]{3,2,1,0:T(8,128)(2,1)S(1)}, bf16[4,1,128,2048]{3,2,1,0:T(8,128)(2,1)}, u32[]{:S(2)}) copy-start(bf16[4,1,128,2048]{3,2,1,0:T(8,128)(2,1)} %shard_map.115) | copy-start | bytes 6291460
  166.6 48.9 %copy-start.15 = (f32[128]{0:T(128)}, f32[128]{0:T(128)S(1)}, u32[]{:S(2)}) copy-start(f32[128]{0:T(128)S(1)} %get-tuple-element.55) | copy-start | bytes 1540
  223.8 1.8 copy-start.10
  223.8 1.8 copy-start.14
  272.9 7.9 %copy-start.13 = (bf16[4,128,256]{2,1,0:T(8,128)(2,1)S(1)}, bf16[4,128,256]{2,1,0:T(8,128)(2,1)}, u32[]{:S(2)}) copy-start(bf16[4,128,256]{2,1,0:T(8,128)(2,1)} %get-tuple-element.22) | copy-start | bytes 786436
  280.8 1.2 copy-start.8
  280.8 1.3 copy-start.12
  345.8 18.7 %copy-start.16 = (f32[128]{0:T(128)S(1)}, f32[128]{0:T(128)}, u32[]{:S(2)}) copy-start(f32[128]{0:T(128)} %copy-done.15) | copy-start | bytes 1540
  345.9 18.7 %copy-start.18 = (f32[128]{0:T(128)S(1)}, f32[128]{0:T(128)}, u32[]{:S(2)}) copy-start(f32[128]{0:T(128)} %get-tuple-element.54) | copy-start | bytes 1540
  364.8 4.6 %copy-start.2 = (bf16[128,2048]{1,0:T(8,128)(2,1)}, bf16[128,2048]{1,0:T(8,128)(2,1)S(1)}, u32[]{:S(2)}) copy-start(bf16[128,2048]{1,0:T(8,128)(2,1)S(1)} %subtract_convert_fusion.refs_1_) | copy-start | bytes 1572868
  369.5 43.4 %copy-start.1 = (bf16[4,128,2048]{2,1,0:T(8,128)(2,1)S(1)}, bf16[4,128,2048]{2,1,0:T(8,128)(2,1)}, u32[]{:S(2)}) copy-start(bf16[4,128,2048]{2,1,0:T(8,128)(2,1)} %shard_map.111) | copy-start | bytes 6291460
  412.9 3.2 copy-start.3
  412.9 3.2 copy-start.4
  416.0 1.6 copy-start.5
  416.0 1.6 copy-start.11
Sparse Core Ops, SparseCore 0:
  9.9 72.4 all-gather.2

commit v2 on v1

v2 whole, which is shorter than its diff:
```python
import functools
import math

import jax
import jax.numpy as jnp
from jax import lax
from jax.experimental import pallas as pl
from jax.experimental.pallas import tpu as pltpu
from jax.sharding import PartitionSpec as P

D = 8192
DH = 128


NORM_EPS = 1e-05
ROPE_BASE = 500000.0
NEG_FILL = -1e30


def rope_tables(segment_row, dim):
    length = segment_row.shape[0]
    positions = jnp.arange(length, dtype=jnp.int32)
    earlier = jnp.sum((segment_row[None, :] < segment_row[:, None]).astype(jnp.int32), axis=1)
    places = (positions - earlier).astype(jnp.float32)
    frequency = jnp.exp(jnp.arange(0, dim, 2).astype(jnp.float32) * (-math.log(ROPE_BASE) / dim))
    angles = places[:, None] * frequency[None, :]
    allowed = (segment_row[None, :] == segment_row[:, None]) & (
        positions[None, :] <= positions[:, None]
    )
    return (jnp.cos(angles), jnp.sin(angles), allowed)


MESH = pl.DeviceIdType.MESH


CHUNKS = 4


def greet(axes):
    barrier = pltpu.get_barrier_semaphore()
    total = 0
    for axis in axes:
        size = lax.axis_size(axis)
        me = lax.axis_index(axis)
        for k in range(1, size):
            peer = lax.rem(me + k, size)
            pl.semaphore_signal(barrier, inc=1, device_id={axis: peer}, device_id_type=MESH)
        total += size - 1
    pl.semaphore_wait(barrier, total)


def sent(source, target, send, recv, place):
    return pltpu.make_async_remote_copy(
        src_ref=source,
        dst_ref=target,
        send_sem=send,
        recv_sem=recv,
        device_id=place,
        device_id_type=MESH,
    )


class Square:
    def __init__(self, axis, source, target, send, recv, own):
        self.axis, self.source, self.target = axis, source, target
        self.send, self.recv, self.own = send, recv, own
        self.me = lax.axis_index(axis)
        x, y = lax.rem(self.me, 2), self.me // 2
        self.near = (2 * y + (1 - x), 2 * (1 - y) + x)
        self.half = source.shape[0] // 2
        self.copies, self.arrivals = [], []

    def part(self, h):
        return pl.ds(h * self.half, self.half)

    def start(self):
        for order in range(2):
            for side in range(2):
                h = order if side == 0 else 1 - order
                copy = sent(
                    self.source.at[self.part(h)],
                    self.target.at[self.me, self.part(h)],
                    self.send.at[2 * side + h],
                    self.recv.at[2 * side + h],
                    {self.axis: self.near[side]},
                )
                copy.start()
                self.copies.append(copy)
        self.local = pltpu.make_async_copy(self.source, self.target.at[self.me], self.own)
        self.local.start()

    def arrival(self, slot, h, number):
        return sent(
            self.source.at[self.part(h)],
            self.target.at[slot, self.part(h)],
            self.send.at[number],
            self.recv.at[number],
            {self.axis: self.near[0]},
        )

    def forward(self):
        for side in range(2):
            h = side
            self.arrival(self.near[side], h, 2 * side + h).wait_recv()
            piece = self.target.at[self.near[side], self.part(h)]
            copy = sent(
                piece, piece, self.send.at[4 + h], self.recv.at[4 + h],
                {self.axis: self.near[1 - side]},
            )
            copy.start()
            self.copies.append(copy)

    def finish(self):
        for side in range(2):
            h = 1 - side
            self.arrival(self.near[side], h, 2 * side + h).wait_recv()
        for h in range(2):
            self.arrival(3 - self.me, h, 4 + h).wait_recv()
        for copy in self.copies:
            copy.wait_send()
        self.local.wait()


class Direct:
    def __init__(self, axis, mode, source, target, send, recv, own):
        self.axis, self.mode, self.source, self.target = axis, mode, source, target
        self.send, self.recv, self.own = send, recv, own
        self.copies = []

    def start(self):
        size, me = lax.axis_size(self.axis), lax.axis_index(self.axis)
        whole = self.mode == "gather"
        for k in range(1, size):
            peer = lax.rem(me + k, size)
            copy = sent(
                self.source if whole else self.source.at[peer],
                self.target.at[me],
                self.send.at[k],
                self.recv.at[k],
                {self.axis: peer},
            )
            copy.start()
            self.copies.append(copy)
        local = pltpu.make_async_copy(
            self.source if whole else self.source.at[me], self.target.at[me], self.own
        )
        local.start()
        self.copies.append(local)

    def forward(self):
        pass

    def finish(self):
        for copy in self.copies:
            copy.wait()


def transfer(axis, mode, *refs):
    if mode == "gather" and axis == "fsdp" and lax.axis_size(axis) == 4:
        return Square(axis, *refs)
    return Direct(axis, mode, *refs)


def exchange_kernel(jobs, *refs):
    count = len(jobs)
    ins, outs, sems = refs[:count], refs[count : 2 * count], refs[2 * count :]
    greet(sorted({axis for axis, _ in jobs}))
    moves = [
        transfer(axis, mode, ins[i], outs[i], *sems[3 * i : 3 * i + 3])
        for i, (axis, mode) in enumerate(jobs)
    ]
    for move in moves:
        move.start()
    for move in moves:
        move.forward()
    for move in moves:
        move.finish()


def job_scratch(axis):
    size = max(lax.axis_size(axis), 6)
    return [
        pltpu.SemaphoreType.DMA((size,)),
        pltpu.SemaphoreType.DMA((size,)),
        pltpu.SemaphoreType.DMA,
    ]


def any_call(kernel, number, shapes, scratch, *values):
    return pl.pallas_call(
        kernel,
        out_shape=shapes,
        in_specs=[pl.BlockSpec(memory_space=pl.ANY)] * len(values),
        out_specs=[pl.BlockSpec(memory_space=pl.ANY)] * len(shapes),
        scratch_shapes=scratch,
        compiler_params=pltpu.CompilerParams(collective_id=number, has_side_effects=True),
    )(*values)


def exchange(number, *work):
    jobs = tuple((axis, mode) for _, axis, mode in work)
    shapes, scratch = [], []
    for value, axis, mode in work:
        size = lax.axis_size(axis)
        shape = (size,) + value.shape if mode == "gather" else value.shape
        shapes.append(jax.ShapeDtypeStruct(shape, value.dtype))
        scratch += job_scratch(axis)
    return any_call(
        functools.partial(exchange_kernel, jobs), number, shapes, scratch,
        *[value for value, _, _ in work],
    )


def code_forward_kernel(chunk_ref, extra_ref, out_ref, extra_out, send, recv, *sems):
    sections, rows, cols = lax.axis_size("section"), lax.axis_size("fsdp"), lax.axis_size("tensor")
    s, f, t = lax.axis_index("section"), lax.axis_index("fsdp"), lax.axis_index("tensor")
    fold = cols // rows
    after, before = lax.rem(s + 1, sections), lax.rem(s + sections - 1, sections)
    barrier = pltpu.get_barrier_semaphore()
    for r in range(rows):
        for u in range(fold):
            pl.semaphore_signal(
                barrier, inc=1, device_id=(before, r, f * fold + u), device_id_type=MESH
            )
    for k in range(1, rows):
        pl.semaphore_signal(
            barrier, inc=1, device_id=(s, lax.rem(f + k, rows), t), device_id_type=MESH
        )
    pl.semaphore_wait(barrier, cols + rows - 1)
    slot = f * fold + lax.rem(t, fold)
    copies = []
    for k in range(cols):
        copy = sent(
            chunk_ref, out_ref.at[slot], send.at[k], recv.at[slot], (after, t // fold, k)
        )
        copy.start()
        copies.append(copy)
    move = transfer("fsdp", "gather", extra_ref, extra_out, *sems)
    move.start()
    move.forward()
    for k in range(cols):
        sent(
            chunk_ref, out_ref.at[k], send.at[k], recv.at[k], (after, t // fold, k)
        ).wait_recv()
    for copy in copies:
        copy.wait_send()
    move.finish()


def code_forward(number, chunk, extra):
    rows, cols = lax.axis_size("fsdp"), lax.axis_size("tensor")
    return any_call(
        code_forward_kernel,
        number,
        [
            jax.ShapeDtypeStruct((cols,) + chunk.shape, chunk.dtype),
            jax.ShapeDtypeStruct((rows,) + extra.shape, extra.dtype),
        ],
        [pltpu.SemaphoreType.DMA((cols,)), pltpu.SemaphoreType.DMA((cols,))]
        + job_scratch("fsdp"),
        chunk,
        extra,
    )


def spread_kernel(
    own_ref, sum_ref, columns_ref, gathered_ref, sums_ref,
    right_send, right_recv, left_send, left_recv, cross_send, cross_recv, own_sem, *sems
):
    rows, cols = lax.axis_size("fsdp"), lax.axis_size("tensor")
    f, t = lax.axis_index("fsdp"), lax.axis_index("tensor")
    fold = cols // rows
    size = own_ref.shape[0] // CHUNKS
    greet(("fsdp", "tensor"))
    sums = Direct("tensor", "gather", sum_ref, sums_ref, *sems)
    sums.start()

    def piece(ref, c):
        return ref.at[pl.ds(c * size, size)]

    def hop(d, c, block, way):
        source = piece(own_ref if d == 0 else gathered_ref.at[block], c)
        send, recv = (right_send, right_recv) if way > 0 else (left_send, left_recv)
        return sent(
            source, piece(gathered_ref.at[block], c), send.at[d, c], recv.at[d + 1, c],
            {"tensor": t + way},
        )

    def arrived(d, c, block, way):
        recv = right_recv if way > 0 else left_recv
        return sent(
            piece(own_ref, c), piece(gathered_ref.at[block], c), right_send.at[d, c],
            recv.at[d, c], {"tensor": lax.rem(t + 1, cols)},
        )

    def cross(source, c, block):
        target = piece(columns_ref.at[f, lax.rem(block, fold)], c)
        there = block // fold
        remote = sent(
            source, target, cross_send.at[block, c],
            cross_recv.at[f, lax.rem(block, fold), c], {"fsdp": there},
        )
        local = pltpu.make_async_copy(source, target, own_sem.at[lax.rem(block, fold), c])
        return there, remote, local

    def each(act):
        for d in range(cols):
            for c in range(CHUNKS):
                if d == 0:
                    act(d, c, t, 0)
                    continue

                @pl.when(t - d >= 0)
                def _():
                    act(d, c, t - d, 1)

                @pl.when(t + d < cols)
                def _():
                    act(d, c, t + d, -1)

    def begin(d, c, block, way):
        if d > 0:
            arrived(d, c, block, way).wait_recv()
        if way >= 0 and d < cols - 1:

            @pl.when(t + 1 < cols)
            def _():
                hop(d, c, block, 1).start()

        if way <= 0 and d < cols - 1:

            @pl.when(t > 0)
            def _():
                hop(d, c, block, -1).start()

        source = piece(own_ref if d == 0 else gathered_ref.at[block], c)
        there, remote, local = cross(source, c, block)

        @pl.when(there != f)
        def _():
            remote.start()

        @pl.when(there == f)
        def _():
            local.start()

    def end(d, c, block, way):
        if way >= 0 and d < cols - 1:

            @pl.when(t + 1 < cols)
            def _():
                hop(d, c, block, 1).wait_send()

        if way <= 0 and d < cols - 1:

            @pl.when(t > 0)
            def _():
                hop(d, c, block, -1).wait_send()

        source = piece(own_ref if d == 0 else gathered_ref.at[block], c)
        there, remote, local = cross(source, c, block)

        @pl.when(there != f)
        def _():
            remote.wait_send()

        @pl.when(there == f)
        def _():
            local.wait()

    each(begin)
    for k in range(1, rows):
        peer = lax.rem(f + k, rows)
        for u in range(fold):
            for c in range(CHUNKS):
                sent(
                    piece(own_ref, c), piece(columns_ref.at[peer, u], c), cross_send.at[0, c],
                    cross_recv.at[peer, u, c], {"fsdp": peer},
                ).wait_recv()
    each(end)
    sums.finish()


def spread(number, own, sums):
    rows, cols = lax.axis_size("fsdp"), lax.axis_size("tensor")
    fold = cols // rows
    dma = pltpu.SemaphoreType.DMA
    return any_call(
        spread_kernel,
        number,
        [
            jax.ShapeDtypeStruct((rows, fold) + own.shape, own.dtype),
            jax.ShapeDtypeStruct((cols,) + own.shape, own.dtype),
            jax.ShapeDtypeStruct((cols,) + sums.shape, sums.dtype),
        ],
        [dma((cols, CHUNKS)) for _ in range(5)]
        + [dma((rows, fold, CHUNKS)), dma((fold, CHUNKS))]
        + job_scratch("tensor"),
        own,
        sums,
    )


def back_kernel(
    in_ref, out_ref, middle_ref, cross_send, cross_recv, send, recv, own_sem
):
    rows, cols = lax.axis_size("fsdp"), lax.axis_size("tensor")
    f, t = lax.axis_index("fsdp"), lax.axis_index("tensor")
    fold = cols // rows
    size = in_ref.shape[2] // CHUNKS
    greet(("fsdp", "tensor"))

    def piece(ref, c):
        return ref.at[pl.ds(c * size, size)]

    def cross(k, u, c):
        peer = lax.rem(f + k, rows)
        return sent(
            piece(in_ref.at[peer, u], c), piece(middle_ref.at[f, u], c),
            cross_send.at[k, u, c], cross_recv.at[k, u, c], {"fsdp": peer},
        )

    def onward(k, u, c):
        origin = lax.rem(f + rows - k, rows)
        block = origin * fold + u
        source = piece((in_ref if k == 0 else middle_ref).at[origin, u], c)
        target = piece(out_ref.at[t], c)
        remote = sent(source, target, send.at[k, u, c], recv.at[t, c], {"tensor": block})
        return block, remote, pltpu.make_async_copy(source, target, own_sem.at[c])

    def landed(k, u, c):
        origin = lax.rem(f + rows - k, rows)
        return sent(
            piece(in_ref.at[origin, u], c), piece(middle_ref.at[origin, u], c),
            cross_send.at[k, u, c], cross_recv.at[k, u, c], {"fsdp": lax.rem(f + k, rows)},
        )

    order = [(k, u, c) for c in range(CHUNKS) for k in range(rows) for u in range(fold)]
    for k, u, c in order:
        if k > 0:
            cross(k, u, c).start()
    for k, u, c in order:
        if k > 0:
            landed(k, u, c).wait_recv()
        block, remote, local = onward(k, u, c)

        @pl.when(block != t)
        def _():
            remote.start()

        @pl.when(block == t)
        def _():
            local.start()

    for k in range(1, cols):
        peer = lax.rem(t + k, cols)
        for c in range(CHUNKS):
            sent(
                piece(in_ref.at[0, 0], c), piece(out_ref.at[peer], c), send.at[0, 0, c],
                recv.at[peer, c], {"tensor": peer},
            ).wait_recv()
    for k, u, c in order:
        if k > 0:
            cross(k, u, c).wait_send()
        block, remote, local = onward(k, u, c)

        @pl.when(block != t)
        def _():
            remote.wait_send()

        @pl.when(block == t)
        def _():
            local.wait()


def back_to_features(number, parts):
    rows, cols = lax.axis_size("fsdp"), lax.axis_size("tensor")
    fold = cols // rows
    dma = pltpu.SemaphoreType.DMA
    return any_call(
        back_kernel,
        number,
        [
            jax.ShapeDtypeStruct((cols,) + parts.shape[2:], parts.dtype),
            jax.ShapeDtypeStruct(parts.shape, parts.dtype),
        ],
        [dma((rows, fold, CHUNKS)) for _ in range(3)]
        + [dma((cols, CHUNKS)), dma((CHUNKS,))],
        parts,
    )[0]


def attend_kernel(
    group_size, query_ref, key_ref, value_ref, up_ref, cos_ref, sin_ref, norm_ref, allowed_ref,
    mixed_ref, query_grad_ref, key_grad_ref, value_grad_ref
):
    low = jnp.bfloat16
    factor = 1.0 / math.sqrt(DH)
    cosine, sine, norm = cos_ref[...], sin_ref[...], norm_ref[...]
    allowed = allowed_ref[...] > 0

    def total(ref, columns):
        parts = ref[0, :, columns].astype(jnp.float32)
        for r in range(1, ref.shape[0]):
            parts += ref[r, :, columns].astype(jnp.float32)
        return parts * norm

    def turned(values):
        return values * cosine + pltpu.roll(values, DH // 2, 1) * sine

    def turned_back(values):
        return values * cosine - pltpu.roll(values, DH // 2, 1) * sine

    key_rot = turned(total(key_ref, pl.ds(0, DH))).astype(low)
    value = total(value_ref, pl.ds(0, DH)).astype(low)
    key_grad = jnp.zeros(key_rot.shape, jnp.float32)
    value_grad = jnp.zeros(key_rot.shape, jnp.float32)
    for h in range(group_size):
        columns = pl.ds(h * DH, DH)
        query_rot = turned(total(query_ref, columns)).astype(low)
        scores = jnp.where(allowed, dot_last(query_rot, key_rot) * factor, NEG_FILL)
        exponent = jnp.exp(scores - jnp.max(scores, axis=-1, keepdims=True))
        probs = exponent / jnp.sum(exponent, axis=-1, keepdims=True)
        probs_low = probs.astype(low)
        upstream = up_ref[:, columns]
        mixed_ref[:, columns] = dot(probs_low, value).astype(low)
        prob_grad = dot_last(upstream, value)
        value_grad += dot_first(probs_low, upstream)
        score_grad = probs * (prob_grad - jnp.sum(probs * prob_grad, axis=-1, keepdims=True))
        score_low = score_grad.astype(low)
        query_grad_ref[:, columns] = turned_back(dot(score_low, key_rot) * factor).astype(low)
        key_grad += dot_first(score_low, query_rot) * factor
    key_grad_ref[...] = turned_back(key_grad).astype(low)
    value_grad_ref[...] = value_grad.astype(low)


def attend(query_parts, key_parts, value_parts, norm_factor, upstream, segment_row):
    rows, tokens, query_width = query_parts.shape
    pair_count = key_parts.shape[2] // DH
    wide = query_width // pair_count
    cosine, sine, allowed = rope_tables(segment_row, DH)
    fixed = pl.BlockSpec((tokens, DH), lambda g: (0, 0))
    parts = pl.BlockSpec((rows, tokens, DH), lambda g: (0, 0, g))
    one = pl.BlockSpec((tokens, DH), lambda g: (0, g))
    group = pl.BlockSpec((tokens, wide), lambda g: (0, g))
    low = jnp.bfloat16
    return pl.pallas_call(
        functools.partial(attend_kernel, wide // DH),
        grid=(pair_count,),
        out_shape=[
            jax.ShapeDtypeStruct((tokens, query_width), low),
            jax.ShapeDtypeStruct((tokens, query_width), low),
            jax.ShapeDtypeStruct((tokens, pair_count * DH), low),
            jax.ShapeDtypeStruct((tokens, pair_count * DH), low),
        ],
        in_specs=[
            pl.BlockSpec((rows, tokens, wide), lambda g: (0, 0, g)),
            parts, parts, group, fixed, fixed, fixed,
            pl.BlockSpec((tokens, tokens), lambda g: (0, 0)),
        ],
        out_specs=[group, group, one, one],
        compiler_params=pltpu.CompilerParams(vmem_limit_bytes=32 * 1024 * 1024),
    )(
        query_parts, key_parts, value_parts, upstream,
        jnp.concatenate([cosine, cosine], axis=1), jnp.concatenate([-sine, sine], axis=1),
        jnp.broadcast_to(norm_factor, (tokens, DH)), allowed.astype(jnp.float32),
    )


def code_back_kernel(chunk_ref, out_ref, send, recv):
    sections, cols = lax.axis_size("section"), lax.axis_size("tensor")
    s, f, t = lax.axis_index("section"), lax.axis_index("fsdp"), lax.axis_index("tensor")
    after, before = lax.rem(s + 1, sections), lax.rem(s + sections - 1, sections)
    barrier = pltpu.get_barrier_semaphore()
    for k in range(cols):
        pl.semaphore_signal(barrier, inc=1, device_id=(after, f, k), device_id_type=MESH)
    pl.semaphore_wait(barrier, cols)
    copies = []
    for k in range(cols):
        copy = pltpu.make_async_remote_copy(
            src_ref=chunk_ref,
            dst_ref=out_ref.at[t],
            send_sem=send.at[k],
            recv_sem=recv.at[t],
            device_id=(before, f, k),
            device_id_type=MESH,
        )
        copy.start()
        copies.append(copy)
    for k in range(cols):
        pltpu.make_async_remote_copy(
            src_ref=chunk_ref,
            dst_ref=out_ref.at[k],
            send_sem=send.at[k],
            recv_sem=recv.at[k],
            device_id=(before, f, k),
            device_id_type=MESH,
        ).wait_recv()
    for copy in copies:
        copy.wait_send()


def code_back(number, chunk):
    cols = lax.axis_size("tensor")
    return pl.pallas_call(
        code_back_kernel,
        out_shape=jax.ShapeDtypeStruct((cols,) + chunk.shape, chunk.dtype),
        in_specs=[pl.BlockSpec(memory_space=pl.ANY)],
        out_specs=pl.BlockSpec(memory_space=pl.ANY),
        scratch_shapes=[pltpu.SemaphoreType.DMA((cols,)), pltpu.SemaphoreType.DMA((cols,))],
        compiler_params=pltpu.CompilerParams(collective_id=number, has_side_effects=True),
    )(chunk)


def dot_last(left, right):
    return lax.dot_general(
        left, right, (((1,), (1,)), ((), ())), preferred_element_type=jnp.float32
    )


def dot_first(left, right):
    return lax.dot_general(
        left, right, (((0,), (0,)), ((), ())), preferred_element_type=jnp.float32
    )


def dot(left, right):
    return jnp.dot(left, right, preferred_element_type=jnp.float32)


def summed(parts):
    return jnp.sum(parts.astype(jnp.float32), axis=0)


def as_rows(row):
    return jnp.broadcast_to(row[None, :], (8, row.shape[0]))


def body(
    hidden,
    encoder_weight,
    decoder_weight,
    query_weight,
    key_weight,
    value_weight,
    segments,
    out_grad,
):
    low = jnp.bfloat16
    rows, cols = lax.axis_size("fsdp"), lax.axis_size("tensor")
    fold = cols // rows
    residual, encoder, decoder = hidden[0], encoder_weight[0], decoder_weight[0]
    wq, wk, wv = query_weight[0], key_weight[0], value_weight[0]
    tokens, width = residual.shape
    code_rows = encoder.shape[0]
    query_width, key_width = wq.shape[1], wk.shape[1]

    (hidden_all,) = exchange(0, (residual, "fsdp", "gather"))
    hidden_all = hidden_all.reshape(rows * tokens, width)
    chunk = rows * tokens // cols
    code_partial = dot_last(hidden_all, encoder).astype(low).reshape(cols, chunk, code_rows)
    split = code_rows // 2
    code_parts, decoder_upper = exchange(
        1, (code_partial, "tensor", "scatter"), (decoder[:split], "fsdp", "gather")
    )
    pieces, decoder_lower = code_forward(2, summed(code_parts).astype(low), decoder[split:])
    decoder_rows = jnp.concatenate([decoder_upper, decoder_lower], axis=1).reshape(-1, width)
    code_received = (
        pieces.reshape(rows, fold, chunk, code_rows)
        .transpose(1, 2, 0, 3)
        .reshape(tokens, rows * code_rows)
    )
    decoded = dot(code_received, decoder_rows)
    square_sum = jnp.sum(decoded * decoded, axis=1)
    columns, _, square_all = spread(3, decoded.astype(low), as_rows(square_sum))
    norm_factor = lax.rsqrt(jnp.sum(square_all[:, 0], axis=0) / D + NORM_EPS)[:, None]
    columns = columns.transpose(0, 2, 1, 3).reshape(rows * tokens, fold * width)
    query_parts, key_parts, value_parts = exchange(
        5,
        (dot(columns, wq).astype(low).reshape(rows, tokens, query_width), "fsdp", "scatter"),
        (dot(columns, wk).astype(low).reshape(rows, tokens, key_width), "fsdp", "scatter"),
        (dot(columns, wv).astype(low).reshape(rows, tokens, key_width), "fsdp", "scatter"),
    )
    query_parts, encoder = lax.optimization_barrier((query_parts, encoder))
    encoder_rows = lax.all_gather(encoder, "fsdp", axis=0, tiled=True)
    mixed, query_grad, key_grad, value_grad = attend(
        query_parts, key_parts, value_parts, norm_factor, out_grad[0], segments[0, 0]
    )
    code_split = code_received.reshape(tokens, rows, code_rows).transpose(1, 0, 2)
    query_grads, key_grads, value_grads, code_all = exchange(
        6,
        (query_grad, "fsdp", "gather"),
        (key_grad, "fsdp", "gather"),
        (value_grad, "fsdp", "gather"),
        (code_split, "fsdp", "scatter"),
    )
    whole = rows * tokens
    partial_cols = (
        dot_last(query_grads.reshape(whole, query_width), wq)
        + dot_last(key_grads.reshape(whole, key_width), wk)
        + dot_last(value_grads.reshape(whole, key_width), wv)
    ).astype(low)
    partial_cols = partial_cols.reshape(rows, tokens, fold, width).transpose(0, 2, 1, 3)
    grad_parts = back_to_features(7, partial_cols)
    normed_grad = summed(grad_parts)
    (inner_parts,) = exchange(
        9, (as_rows(jnp.sum(normed_grad * decoded, axis=1)), "tensor", "gather")
    )
    inner_dot = jnp.sum(inner_parts[:, 0], axis=0)[:, None]
    decoded_grad = (norm_factor * normed_grad - decoded * norm_factor**3 * inner_dot / D).astype(
        low
    )
    grad_partial = dot_last(decoded_grad, decoder_rows).astype(low)
    code_grad_parts, decoded_grads = exchange(
        10,
        (grad_partial.reshape(cols, tokens // cols, rows * code_rows), "tensor", "scatter"),
        (decoded_grad, "fsdp", "gather"),
    )
    code_grad = code_back(11, summed(code_grad_parts).astype(low))
    code_grad = code_grad.reshape(tokens, rows * code_rows)
    (code_grads,) = exchange(
        12, (code_grad.reshape(tokens, rows, code_rows).transpose(1, 0, 2), "fsdp", "scatter")
    )
    hidden_grad = dot(code_grad, encoder_rows).astype(low)
    decoder_grad = dot_first(
        code_all.reshape(whole, code_rows), decoded_grads.reshape(whole, width)
    )
    encoder_grad = dot_first(code_grads.reshape(whole, code_rows), hidden_all)
    return (mixed[None], hidden_grad[None], encoder_grad[None], decoder_grad[None])


def solution(mesh):
    placed = (
        P("section", "fsdp", "tensor"),
        P("section", "fsdp", "tensor"),
        P("section", "fsdp", "tensor"),
        P("section", "fsdp", "tensor"),
        P("section", "fsdp", "tensor"),
        P("section", "fsdp", "tensor"),
        P("section", "fsdp", None),
        P("section", "fsdp", "tensor"),
    )
    return jax.shard_map(
        body,
        mesh=mesh,
        in_specs=placed,
        out_specs=(
            P("section", "fsdp", "tensor"),
            P("section", "fsdp", "tensor"),
            P("section", "fsdp", "tensor"),
            P("section", "fsdp", "tensor"),
        ),
        check_vma=False,
    )
```

time: 427 us -> 372 us (0.87)
  Pallas kernels: 318 us -> 293 us
  matrix products: 52.2 us -> 40.9 us
  waiting for transfers between devices: 8.49 us -> 0.02 us
  local copies, waits for them, and re-layouts: 17.3 us -> 12 us
  other arithmetic: 15.5 us -> 10.8 us
    pallas_call x12 -> x11, Pallas kernels: 310 us -> 285 us  [the longest x10 274 us: any_call(): pl.pallas_call(kernel, out_shape=shapes, in_specs=[pl.BlockSpec(memory_sp...]
    all_gather x1, waiting for transfers between devices: 7.81 us -> 0.01 us  [body(): encoder_rows = lax.all_gather(encoder, 'fsdp', axis=0, tiled=True)]
    dot_general x5 -> x0, matrix products: 7.56 us -> none  [product(): return jnp.einsum(form, left, right, preferred_element_type=jnp.float32)]
    reduce_sum x5 -> x3, other arithmetic: 8.57 us -> 5.34 us  [summed(): return jnp.sum(parts.astype(jnp.float32), axis=0)]
  transfers between devices with their start and end apart: 1 -> 1, of which waited for: 1 -> 0; matrix products, arithmetic and copies ran while one was open for 2% -> 8% of each run, Pallas kernels for 14% -> 38%
where the time goes in v2:
time: 372 us; the launch traced here: 371 us
  Pallas kernels  293 us (79%)
  matrix products  40.9 us (11%)
  between operations  14.4 us (4%)
  local copies, waits for them, and re-layouts  12 us (3%)
  other arithmetic  10.8 us (3%)
    pallas_call x10, Pallas kernels, any_call(): pl.pallas_call(kernel, out_shape=shapes, in_specs=[pl.BlockSpec(memory_sp...  274 us
    dot_general x5, matrix products, dot(): return jnp.dot(left, right, preferred_element_type=jnp.float32)  18.6 us
    dot_general x5, matrix products, dot_last(): lax.dot_general(left, right, (((1,), (1,)), ((), ())), preferred_element_...  17.1 us
    pallas_call x1, Pallas kernels, attend(): pl.pallas_call(functools.partial(attend_kernel, wide // DH), grid=(pair_c...  10.7 us
    pallas_call x1, Pallas kernels, code_back(): pl.pallas_call(code_back_kernel, out_shape=jax.ShapeDtypeStruct((cols,) +...  8.35 us
  transfers between devices with their start and end apart: 1, of which 0 were waited for; matrix products, arithmetic and copies ran while one was open for 8% of the time, Pallas kernels for 38%

profile of v2, /device:TPU:0, one launch (start us, length us, event | category | flops | bytes accessed | tf_op | source)
XLA Modules:
  0.0 371.1 jit_solution(3427224661746965104)
XLA Ops:
  7.2 22.2 %shard_map.111 = bf16[4,128,2048]{2,1,0:T(8,128)(2,1)} custom-call(bf16[128,2048]{1,0:T(8,128)(2,1)} %bitcast.85), custom_call_target="tpu_custom_call" | custom-call | tf_op jit(solution)/shard_map/pallas_call | solution.py:190
  32.9 22.8 %shard_map.112 = (bf16[4,128,256]{2,1,0:T(8,128)(2,1)}, bf16[4,128,2048]{2,1,0:T(8,128)(2,1)}) custom-call(bf16[4,128,256]{2,1,0:T(8,128)(2,1)} %bitcast.89, bf16[128,2048]{1,0:T(8,128)(2,1)} %get-tuple-element.51.refs_1_), custom_call_target="tpu_custom_call" | custom-call | tf_op jit(solution)/shard_map/pallas_call | solution.py:190
  57.3 24.1 %shard_map.113 = (bf16[4,128,256]{2,1,0:T(8,128)(2,1)}, bf16[4,128,2048]{2,1,0:T(8,128)(2,1)}) custom-call(bf16[128,256]{1,0:T(8,128)(2,1)} %reduce_sum.78.chunk_ref, bf16[128,2048]{1,0:T(8,128)(2,1)} %get-tuple-element.50.extra_ref), custom_call_target="tpu_custom_call" | custom-call | tf_op jit(solution)/shard_map/pallas_call | solution.py:190
  82.5 2.8 pad_maximum_fusion
  85.4 2.0 multiply_reduce_fusion.1
  88.1 42.1 %shard_map.114 = (bf16[4,1,128,2048]{3,2,1,0:T(8,128)(2,1)}, bf16[4,128,2048]{2,1,0:T(8,128)(2,1)}, f32[4,8,128]{2,1,0:T(8,128)}) custom-call(bf16[128,2048]{1,0:T(8,128)(2,1)} %get-tuple-element.49.own_ref, f32[8,128]{1,0:T(8,128)} %broadcast_in_dim.14.sum_ref), custom_call_target="tpu_custom_call" | custom-call | tf_op jit(solution)/shard_map/pallas_call | solution.py:190
  130.2 10.0 %fusion.4 = bf16[512,2048]{1,0:T(8,128)(2,1)} fusion(bf16[512,2048]{1,0:T(8,128)(2,1)} %bitcast.94, bf16[1,2048,2048]{2,1,0:T(8,128)(2,1)} %param.11), kind=kOutput, calls=%fused_computation.7 | convolution fusion | flops 4296015872 | bytes 12582912 | tf_op jit(solution)/shard_map/dot_general | solution.py:628
  143.0 42.2 %shard_map.115 = (bf16[4,128,2048]{2,1,0:T(8,128)(2,1)}, bf16[4,128,256]{2,1,0:T(8,128)(2,1)}, bf16[4,128,256]{2,1,0:T(8,128)(2,1)}) custom-call(bf16[4,128,2048]{2,1,0:T(8,128)(2,1)} %bitcast.79, bf16[4,128,256]{2,1,0:T(8,128)(2,1)} %bitcast.87, bf16[4,128,256]{2,1,0:T(8,128)(2,1)} %bitcast.88), custom_call_target="tpu_custom_call" | custom-call | tf_op jit(solution)/shard_map/pallas_call | solution.py:190
  190.4 10.7 %shard_map.116 = (bf16[128,2048]{1,0:T(8,128)(2,1)}, bf16[128,2048]{1,0:T(8,128)(2,1)S(1)}, bf16[128,256]{1,0:T(8,128)(2,1)S(1)}, bf16[128,256]{1,0:T(8,128)(2,1)S(1)}) custom-call(bf16[4,128,2048]{2,1,0:T(8,128)(2,1)S(1)} %copy-done.2, bf16[4,128,256]{2,1,0:T(8,128)(2,1)S(1)} %copy-done.5, bf16[4,128,256]{2,1,0:T(8,128)(2,1)S(1)} %copy-done.6, ...), custom_call_target="tpu_custom_call" | custom-call | tf_op jit(solution)/shard_map/pallas_call | solution.py:547
  203.1 35.7 %shard_map.117 = (bf16[4,128,2048]{2,1,0:T(8,128)(2,1)}, bf16[4,128,256]{2,1,0:T(8,128)(2,1)}, bf16[4,128,256]{2,1,0:T(8,128)(2,1)}, bf16[4,128,256]{2,1,0:T(8,128)(2,1)}) custom-call(bf16[128,2048]{1,0:T(8,128)(2,1)} %copy-done.3, bf16[128,256]{1,0:T(8,128)(2,1)} %copy-done.7, bf16[128,256]{1,0:T(8,128)(2,1)} %copy-done.8, ...), custom_call_target="tpu_custom_call" | custom-call | tf_op jit(solution)/shard_map/pallas_call | solution.py:190
  238.8 1.8 fusion.10
  240.7 7.1 %fusion = f32[512,2048]{1,0:T(8,128)S(1)} fusion(bf16[512,2048]{1,0:T(8,128)(2,1)S(1)} %bitcast.93, bf16[1,2048,2048]{2,1,0:T(8,128)(2,1)} %param.11), kind=kOutput, calls=%fused_computation | convolution fusion | flops 4294967296 | bytes 14680064 | tf_op jit(solution)/shard_map/dot_general | solution.py:616
  247.8 2.1 add_convert_fusion
  249.9 47.6 %shard_map.118 = (bf16[4,128,2048]{2,1,0:T(8,128)(2,1)}, bf16[4,1,128,2048]{3,2,1,0:T(8,128)(2,1)}) custom-call(bf16[4,1,128,2048]{3,2,1,0:T(8,128)(2,1)} %bitcast.77), custom_call_target="tpu_custom_call" | custom-call | tf_op jit(solution)/shard_map/pallas_call | solution.py:190
  297.5 2.1 convert_reduce_fusion
  300.4 9.3 %shard_map.119 = f32[4,8,128]{2,1,0:T(8,128)} custom-call(f32[8,128]{1,0:T(8,128)} %broadcast_in_dim.17.refs_0_), custom_call_target="tpu_custom_call" | custom-call | tf_op jit(solution)/shard_map/pallas_call | solution.py:190
  310.7 4.6 %convolution_convert_fusion.4 = bf16[128,1024]{1,0:T(8,128)(2,1)} fusion(bf16[128,2048]{1,0:T(8,128)(2,1)S(1)} %subtract_convert_fusion.refs_1_, bf16[1024,2048]{1,0:T(8,128)(2,1)} %bitcast.75), kind=kOutput, calls=%fused_computation.15 | convolution fusion | flops 537001984 | bytes 4980736 | tf_op jit(solution)/shard_map/dot_general | solution.py:616
  315.3 21.6 %shard_map.120 = (bf16[4,32,1024]{2,1,0:T(8,128)(2,1)}, bf16[4,128,2048]{2,1,0:T(8,128)(2,1)}) custom-call(bf16[4,32,1024]{2,1,0:T(8,128)(2,1)} %bitcast.80, bf16[128,2048]{1,0:T(8,128)(2,1)} %copy-done.12), custom_call_target="tpu_custom_call" | custom-call | tf_op jit(solution)/shard_map/pallas_call | solution.py:190
  337.0 1.6 reduce_sum.85.chunk_ref
  338.6 8.4 %shard_map.121 = bf16[4,32,1024]{2,1,0:T(8,128)(2,1)} custom-call(bf16[32,1024]{1,0:T(8,128)(2,1)} %reduce_sum.85.chunk_ref), custom_call_target="tpu_custom_call" | custom-call | tf_op jit(solution)/shard_map/pallas_call | solution.py:605
  348.9 6.3 %shard_map.122 = bf16[4,128,256]{2,1,0:T(8,128)(2,1)} custom-call(bf16[4,128,256]{2,1,0:T(8,128)(2,1)} %bitcast.84), custom_call_target="tpu_custom_call" | custom-call | tf_op jit(solution)/shard_map/pallas_call | solution.py:190
  355.2 3.1 convolution_bitcast_fusion.1
  358.4 2.0 convolution_bitcast_fusion
  360.5 3.8 %fusion.7 = bf16[1,128,2048]{2,1,0:T(8,128)(2,1)} fusion(bf16[128,1024]{1,0:T(8,128)(2,1)S(1)} %bitcast.78, bf16[1024,2048]{1,0:T(8,128)(2,1)} %all-gather.2.cloned.1.call-done), kind=kOutput, calls=%fused_computation.11 | convolution fusion | flops 537133056 | bytes 4980736 | tf_op jit(solution)/shard_map/dot_general | solution.py:628
  (73 shorter events, 20.6 us)
Async XLA Ops:
  7.2 133.0 %copy-start = (bf16[1,2048,256]{2,1,0:T(8,128)(2,1)S(1)}, bf16[1,2048,256]{2,1,0:T(8,128)(2,1)}, u32[]{:S(2)}) copy-start(bf16[1,2048,256]{2,1,0:T(8,128)(2,1)} %param.12) | copy-start | bytes 3145732
  7.2 22.3 %copy-start.17 = (bf16[1,256,2048]{2,1,0:T(8,128)(2,1)S(1)}, bf16[1,256,2048]{2,1,0:T(8,128)(2,1)}, u32[]{:S(2)}) copy-start(bf16[1,256,2048]{2,1,0:T(8,128)(2,1)} %param.10) | copy-start | bytes 3145732
  7.2 353.3 %all-gather.2.cloned.1.call-start = ((), (), s32[]{:S(2)}) async-start(), calls=%async_computation | async-start | bytes 5242880 | tf_op jit(solution)/shard_map/all_gather | solution.py:685
  7.2 23.3 %copy-start.18 = (bf16[1,256,2048]{2,1,0:T(8,128)(2,1)S(1)}, bf16[1,256,2048]{2,1,0:T(8,128)(2,1)}, u32[]{:S(2)}) copy-start(bf16[1,256,2048]{2,1,0:T(8,128)(2,1)} %param.9) | copy-start | bytes 3145732
  29.5 2.0 copy-start.10
  85.3 2.1 copy-start.9
  130.2 10.0 %copy-start.23 = (bf16[4,1,128,2048]{3,2,1,0:T(8,128)(2,1)S(1)}, bf16[4,1,128,2048]{3,2,1,0:T(8,128)(2,1)}, u32[]{:S(2)}) copy-start(bf16[4,1,128,2048]{3,2,1,0:T(8,128)(2,1)} %get-tuple-element.30) | copy-start | bytes 6291460
  140.2 1.4 copy-start.15
  143.0 43.0 %copy-start.21 = (s32[1,1,128]{2,1,0:T(1,128)S(1)}, s32[1,1,128]{2,1,0:T(1,128)}, u32[]{:S(2)}) copy-start(s32[1,1,128]{2,1,0:T(1,128)} %param.14) | copy-start | bytes 1540
  143.0 43.8 %copy-start.4 = (bf16[1,128,2048]{2,1,0:T(8,128)(2,1)S(1)}, bf16[1,128,2048]{2,1,0:T(8,128)(2,1)}, u32[]{:S(2)}) copy-start(bf16[1,128,2048]{2,1,0:T(8,128)(2,1)} %param.15) | copy-start | bytes 1572868
  186.8 1.6 copy-start.2
  188.4 0.9 copy-start.5
  189.4 1.0 copy-start.6
  201.0 0.8 copy-start.3
  201.8 0.6 copy-start.7
  238.8 1.9 copy-start.22
  240.7 7.1 %copy-start.16 = (bf16[1,2048,256]{2,1,0:T(8,128)(2,1)S(1)}, bf16[1,2048,256]{2,1,0:T(8,128)(2,1)}, u32[]{:S(2)}) copy-start(bf16[1,2048,256]{2,1,0:T(8,128)(2,1)} %param.13) | copy-start | bytes 3145732
  240.7 7.1 %copy-start.20 = (bf16[4,128,256]{2,1,0:T(8,128)(2,1)S(1)}, bf16[4,128,256]{2,1,0:T(8,128)(2,1)}, u32[]{:S(2)}) copy-start(bf16[4,128,256]{2,1,0:T(8,128)(2,1)} %get-tuple-element.42) | copy-start | bytes 786436
  310.7 4.6 %copy-start.12 = (bf16[128,2048]{1,0:T(8,128)(2,1)}, bf16[128,2048]{1,0:T(8,128)(2,1)S(1)}, u32[]{:S(2)}) copy-start(bf16[128,2048]{1,0:T(8,128)(2,1)S(1)} %subtract_convert_fusion.refs_1_) | copy-start | bytes 1572868
  315.3 39.9 %copy-start.11 = (bf16[4,128,2048]{2,1,0:T(8,128)(2,1)S(1)}, bf16[4,128,2048]{2,1,0:T(8,128)(2,1)}, u32[]{:S(2)}) copy-start(bf16[4,128,2048]{2,1,0:T(8,128)(2,1)} %shard_map.111) | copy-start | bytes 6291460
  355.2 3.2 copy-start.14
  355.2 3.2 copy-start.19
  358.4 2.1 copy-start.13
  360.5 3.8 %copy-start.1 = (bf16[1,2048,256]{2,1,0:T(8,128)(2,1)S(1)}, bf16[1,2048,256]{2,1,0:T(8,128)(2,1)}, u32[]{:S(2)}) copy-start(bf16[1,2048,256]{2,1,0:T(8,128)(2,1)} %param.12) | copy-start | bytes 3145732
  (1 other events, 0.6 us)
Sparse Core Ops, SparseCore 0:
  185.4 69.6 all-gather.1

commit v3 on v2

--- a/solution.py
+++ b/solution.py
@@ -402,46 +402,64 @@
 
 
 def back_kernel(
-    in_ref, out_ref, middle_ref, cross_send, cross_recv, send, recv, own_sem
+    *refs
 ):
+    grads, weights, code_ref, (out_ref, code_out) = refs[:3], refs[3:6], refs[6], refs[7:9]
+    held, loaded, (product_ref, middle_ref) = refs[9:12], refs[12:15], refs[15:17]
+    gather_send, gather_recv, load_sem = refs[17:20]
+    cross_send, cross_recv, send, recv, own_sem = refs[20:25]
+    code_sems = refs[25:]
     rows, cols = lax.axis_size("fsdp"), lax.axis_size("tensor")
     f, t = lax.axis_index("fsdp"), lax.axis_index("tensor")
     fold = cols // rows
-    size = in_ref.shape[2] // CHUNKS
+    width = product_ref.shape[3]
+    size = product_ref.shape[2] // CHUNKS
+    order = [0, 2, 1, 3] if rows == 4 else list(range(rows))
+    loads = [
+        pltpu.make_async_copy(weights[i], loaded[i], load_sem.at[i]) for i in range(3)
+    ]
+    owns = [
+        pltpu.make_async_copy(grads[i], held[i].at[0], load_sem.at[3 + i]) for i in range(3)
+    ]
+    for copy in loads + owns:
+        copy.start()
     greet(("fsdp", "tensor"))
+
+    def away(k):
+        return lax.rem(f + k, rows)
+
+    def origin(k):
+        return lax.rem(f + rows - k, rows)
+
+    def spread_out(k, i):
+        return sent(
+            grads[i], held[i].at[k], gather_send.at[i, k], gather_recv.at[i, k],
+            {"fsdp": away(k)},
+        )
+
+    for k in order[1:]:
+        for i in range(3):
+            spread_out(k, i).start()
+    codes = Direct("fsdp", "scatter", code_ref, code_out, *code_sems)
+    codes.start()
 
     def piece(ref, c):
         return ref.at[pl.ds(c * size, size)]
 
     def cross(k, u, c):
-        peer = lax.rem(f + k, rows)
         return sent(
-            piece(in_ref.at[peer, u], c), piece(middle_ref.at[f, u], c),
-            cross_send.at[k, u, c], cross_recv.at[k, u, c], {"fsdp": peer},
+            piece(product_ref.at[k, u], c), piece(middle_ref.at[k, u], c),
+            cross_send.at[k, u, c], cross_recv.at[k, u, c], {"fsdp": origin(k)},
         )
 
     def onward(k, u, c):
-        origin = lax.rem(f + rows - k, rows)
-        block = origin * fold + u
-        source = piece((in_ref if k == 0 else middle_ref).at[origin, u], c)
+        block = away(k) * fold + u
+        source = piece((product_ref if k == 0 else middle_ref).at[k, u], c)
         target = piece(out_ref.at[t], c)
         remote = sent(source, target, send.at[k, u, c], recv.at[t, c], {"tensor": block})
         return block, remote, pltpu.make_async_copy(source, target, own_sem.at[c])
 
-    def landed(k, u, c):
-        origin = lax.rem(f + rows - k, rows)
-        return sent(
-            piece(in_ref.at[origin, u], c), piece(middle_ref.at[origin, u], c),
-            cross_send.at[k, u, c], cross_recv.at[k, u, c], {"fsdp": lax.rem(f + k, rows)},
-        )
-
-    order = [(k, u, c) for c in range(CHUNKS) for k in range(rows) for u in range(fold)]
-    for k, u, c in order:
-        if k > 0:
-            cross(k, u, c).start()
-    for k, u, c in order:
-        if k > 0:
-            landed(k, u, c).wait_recv()
+    def pass_on(k, u, c):
         block, remote, local = onward(k, u, c)
 
         @pl.when(block != t)
@@ -452,42 +470,87 @@
         def _():
             local.start()
 
+    for copy in loads + owns:
+        copy.wait()
+    tile = min(width, 512)
+    for k in order:
+        if k > 0:
+            for i in range(3):
+                spread_out(k, i).wait_recv()
+        for u in range(fold):
+
+            @pl.loop(0, width // tile)
+            def _(n):
+                lower = pl.multiple_of(u * width + n * tile, tile)
+                total = dot_last(held[0][k], loaded[0][pl.ds(lower, tile), :])
+                for i in range(1, 3):
+                    total += dot_last(held[i][k], loaded[i][pl.ds(lower, tile), :])
+                columns = pl.ds(pl.multiple_of(n * tile, tile), tile)
+                product_ref[k, u, :, columns] = total.astype(product_ref.dtype)
+
+            for c in range(CHUNKS):
+                if k == 0:
+                    pass_on(k, u, c)
+                else:
+                    cross(k, u, c).start()
+    for k in order[1:]:
+        for u in range(fold):
+            for c in range(CHUNKS):
+                cross(k, u, c).wait_recv()
+                pass_on(k, u, c)
     for k in range(1, cols):
         peer = lax.rem(t + k, cols)
         for c in range(CHUNKS):
             sent(
-                piece(in_ref.at[0, 0], c), piece(out_ref.at[peer], c), send.at[0, 0, c],
+                piece(middle_ref.at[0, 0], c), piece(out_ref.at[peer], c), send.at[0, 0, c],
                 recv.at[peer, c], {"tensor": peer},
             ).wait_recv()
-    for k, u, c in order:
-        if k > 0:
-            cross(k, u, c).wait_send()
-        block, remote, local = onward(k, u, c)
-
-        @pl.when(block != t)
-        def _():
-            remote.wait_send()
-
-        @pl.when(block == t)
-        def _():
-            local.wait()
-
-
-def back_to_features(number, parts):
+    for k in order:
+        for i in range(3):
+            if k > 0:
+                spread_out(k, i).wait_send()
+        for u in range(fold):
+            for c in range(CHUNKS):
+                if k > 0:
+                    cross(k, u, c).wait_send()
+                block, remote, local = onward(k, u, c)
+
+                @pl.when(block != t)
+                def _():
+                    remote.wait_send()
+
+                @pl.when(block == t)
+                def _():
+                    local.wait()
+
+    codes.finish()
+
+
+def back_to_features(number, grads, weights, codes):
     rows, cols = lax.axis_size("fsdp"), lax.axis_size("tensor")
     fold = cols // rows
     dma = pltpu.SemaphoreType.DMA
-    return any_call(
+    tokens, low = grads[0].shape[0], jnp.bfloat16
+    width = weights[0].shape[0] // fold
+    return pl.pallas_call(
         back_kernel,
-        number,
-        [
-            jax.ShapeDtypeStruct((cols,) + parts.shape[2:], parts.dtype),
-            jax.ShapeDtypeStruct(parts.shape, parts.dtype),
+        out_shape=[
+            jax.ShapeDtypeStruct((cols, tokens, width), low),
+            jax.ShapeDtypeStruct(codes.shape, codes.dtype),
         ],
-        [dma((rows, fold, CHUNKS)) for _ in range(3)]
-        + [dma((cols, CHUNKS)), dma((CHUNKS,))],
-        parts,
-    )[0]
+        in_specs=[pl.BlockSpec(memory_space=pl.ANY)] * 7,
+        out_specs=[pl.BlockSpec(memory_space=pl.ANY)] * 2,
+        scratch_shapes=[pltpu.VMEM((rows,) + grad.shape, low) for grad in grads]
+        + [pltpu.VMEM(weight.shape, low) for weight in weights]
+        + [pltpu.VMEM((rows, fold, tokens, width), low)] * 2
+        + [dma((3, rows)), dma((3, rows)), dma((6,))]
+        + [dma((rows, fold, CHUNKS)) for _ in range(3)]
+        + [dma((cols, CHUNKS)), dma((CHUNKS,))]
+        + job_scratch("fsdp"),
+        compiler_params=pltpu.CompilerParams(
+            collective_id=number, has_side_effects=True, vmem_limit_bytes=40 * 1024 * 1024
+        ),
+    )(*grads, *weights, codes)
 
 
 def attend_kernel(
@@ -567,49 +630,59 @@
     )
 
 
-def code_back_kernel(chunk_ref, out_ref, send, recv):
-    sections, cols = lax.axis_size("section"), lax.axis_size("tensor")
+def code_back_kernel(chunk_ref, split_ref, out_ref, rows_out, send, recv, row_send, row_recv):
+    sections, rows, cols = lax.axis_size("section"), lax.axis_size("fsdp"), lax.axis_size("tensor")
     s, f, t = lax.axis_index("section"), lax.axis_index("fsdp"), lax.axis_index("tensor")
     after, before = lax.rem(s + 1, sections), lax.rem(s + sections - 1, sections)
     barrier = pltpu.get_barrier_semaphore()
+    for r in range(rows):
+        for k in range(cols):
+            pl.semaphore_signal(barrier, inc=1, device_id=(after, r, k), device_id_type=MESH)
+    pl.semaphore_wait(barrier, rows * cols)
+    copies, arrivals = [], []
     for k in range(cols):
-        pl.semaphore_signal(barrier, inc=1, device_id=(after, f, k), device_id_type=MESH)
-    pl.semaphore_wait(barrier, cols)
-    copies = []
-    for k in range(cols):
-        copy = pltpu.make_async_remote_copy(
-            src_ref=chunk_ref,
-            dst_ref=out_ref.at[t],
-            send_sem=send.at[k],
-            recv_sem=recv.at[t],
-            device_id=(before, f, k),
-            device_id_type=MESH,
-        )
+        copies.append(
+            sent(chunk_ref, out_ref.at[t], send.at[k], recv.at[t], (before, f, k))
+        )
+        arrivals.append(
+            sent(chunk_ref, out_ref.at[k], send.at[k], recv.at[k], (before, f, k))
+        )
+        for r in range(rows):
+            copies.append(
+                sent(
+                    split_ref.at[r], rows_out.at[f, t], row_send.at[r, k], row_recv.at[f, t],
+                    (before, r, k),
+                )
+            )
+            arrivals.append(
+                sent(
+                    split_ref.at[r], rows_out.at[r, k], row_send.at[r, k], row_recv.at[r, k],
+                    (before, r, k),
+                )
+            )
+    for copy in copies:
         copy.start()
-        copies.append(copy)
-    for k in range(cols):
-        pltpu.make_async_remote_copy(
-            src_ref=chunk_ref,
-            dst_ref=out_ref.at[k],
-            send_sem=send.at[k],
-            recv_sem=recv.at[k],
-            device_id=(before, f, k),
-            device_id_type=MESH,
-        ).wait_recv()
+    for copy in arrivals:
+        copy.wait_recv()
     for copy in copies:
         copy.wait_send()
 
 
 def code_back(number, chunk):
-    cols = lax.axis_size("tensor")
-    return pl.pallas_call(
+    rows, cols = lax.axis_size("fsdp"), lax.axis_size("tensor")
+    dma = pltpu.SemaphoreType.DMA
+    split = chunk.reshape(chunk.shape[0], rows, -1).transpose(1, 0, 2)
+    return any_call(
         code_back_kernel,
-        out_shape=jax.ShapeDtypeStruct((cols,) + chunk.shape, chunk.dtype),
-        in_specs=[pl.BlockSpec(memory_space=pl.ANY)],
-        out_specs=pl.BlockSpec(memory_space=pl.ANY),
-        scratch_shapes=[pltpu.SemaphoreType.DMA((cols,)), pltpu.SemaphoreType.DMA((cols,))],
-        compiler_params=pltpu.CompilerParams(collective_id=number, has_side_effects=True),
-    )(chunk)
+        number,
+        [
+            jax.ShapeDtypeStruct((cols,) + chunk.shape, chunk.dtype),
+            jax.ShapeDtypeStruct((rows, cols) + split.shape[1:], chunk.dtype),
+        ],
+        [dma((cols,)), dma((cols,)), dma((rows, cols)), dma((rows, cols))],
+        chunk,
+        split,
+    )
 
 
 def dot_last(left, right):
@@ -687,21 +760,10 @@
         query_parts, key_parts, value_parts, norm_factor, out_grad[0], segments[0, 0]
     )
     code_split = code_received.reshape(tokens, rows, code_rows).transpose(1, 0, 2)
-    query_grads, key_grads, value_grads, code_all = exchange(
-        6,
-        (query_grad, "fsdp", "gather"),
-        (key_grad, "fsdp", "gather"),
-        (value_grad, "fsdp", "gather"),
-        (code_split, "fsdp", "scatter"),
+    grad_parts, code_all = back_to_features(
+        6, (query_grad, key_grad, value_grad), (wq, wk, wv), code_split
     )
     whole = rows * tokens
-    partial_cols = (
-        dot_last(query_grads.reshape(whole, query_width), wq)
-        + dot_last(key_grads.reshape(whole, key_width), wk)
-        + dot_last(value_grads.reshape(whole, key_width), wv)
-    ).astype(low)
-    partial_cols = partial_cols.reshape(rows, tokens, fold, width).transpose(0, 2, 1, 3)
-    grad_parts = back_to_features(7, partial_cols)
     normed_grad = summed(grad_parts)
     (inner_parts,) = exchange(
         9, (as_rows(jnp.sum(normed_grad * decoded, axis=1)), "tensor", "gather")
@@ -716,11 +778,8 @@
         (grad_partial.reshape(cols, tokens // cols, rows * code_rows), "tensor", "scatter"),
         (decoded_grad, "fsdp", "gather"),
     )
-    code_grad = code_back(11, summed(code_grad_parts).astype(low))
+    code_grad, code_grads = code_back(11, summed(code_grad_parts).astype(low))
     code_grad = code_grad.reshape(tokens, rows * code_rows)
-    (code_grads,) = exchange(
-        12, (code_grad.reshape(tokens, rows, code_rows).transpose(1, 0, 2), "fsdp", "scatter")
-    )
     hidden_grad = dot(code_grad, encoder_rows).astype(low)
     decoder_grad = dot_first(
         code_all.reshape(whole, code_rows), decoded_grads.reshape(whole, width)

time: 372 us -> 380 us (1.022)
  Pallas kernels: 293 us -> 313 us
  matrix products: 40.9 us -> 30.2 us
    pallas_call x1, Pallas kernels: 8.35 us -> 94.7 us  [back_to_features(): pl.pallas_call(back_kernel, out_shape=[jax.ShapeDtypeStruct((cols, tokens...]
    pallas_call x10 -> x8, Pallas kernels: 274 us -> 208 us  [any_call(): pl.pallas_call(kernel, out_shape=shapes, in_specs=[pl.BlockSpec(memory_sp...]
    dot_general x5 -> x2, matrix products: 17.1 us -> 6.11 us  [dot_last(): lax.dot_general(left, right, (((1,), (1,)), ((), ())), preferred_element_...]
    unnamed x48 -> x40, local copies, waits for them, and re-layouts: 6.64 us -> 8.8 us
  transfers between devices with their start and end apart: 1 -> 1, of which waited for: 0 -> 0; matrix products, arithmetic and copies ran while one was open for 8% -> 4% of each run, Pallas kernels for 38% -> 42%
where the time goes in v3:
time: 380 us; the launch traced here: 379 us
  Pallas kernels  313 us (82%)
  matrix products  30.2 us (8%)
  between operations  14.3 us (4%)
  local copies, waits for them, and re-layouts  12.9 us (3%)
  other arithmetic  8.48 us (2%)
    pallas_call x8, Pallas kernels, any_call(): pl.pallas_call(kernel, out_shape=shapes, in_specs=[pl.BlockSpec(memory_sp...  208 us
    pallas_call x1, Pallas kernels, back_to_features(): pl.pallas_call(back_kernel, out_shape=[jax.ShapeDtypeStruct((cols, tokens...  94.7 us
    dot_general x5, matrix products, dot(): return jnp.dot(left, right, preferred_element_type=jnp.float32)  18.9 us
    pallas_call x1, Pallas kernels, attend(): pl.pallas_call(functools.partial(attend_kernel, wide // DH), grid=(pair_c...  10.7 us
    unnamed x40, local copies, waits for them, and re-layouts  8.8 us
  transfers between devices with their start and end apart: 1, of which 0 were waited for; matrix products, arithmetic and copies ran while one was open for 4% of the time, Pallas kernels for 42%

profile of v3, /device:TPU:0, one launch (start us, length us, event | category | flops | bytes accessed | tf_op | source)
XLA Modules:
  0.0 379.0 jit_solution(15230930572814110755)
XLA Ops:
  7.2 22.2 %shard_map.111 = bf16[4,128,2048]{2,1,0:T(8,128)(2,1)} custom-call(bf16[128,2048]{1,0:T(8,128)(2,1)} %bitcast.76), custom_call_target="tpu_custom_call" | custom-call | tf_op jit(solution)/shard_map/pallas_call | solution.py:190
  31.4 1.4 convolution_convert_fusion.4
  32.9 22.8 %shard_map.112 = (bf16[4,128,256]{2,1,0:T(8,128)(2,1)}, bf16[4,128,2048]{2,1,0:T(8,128)(2,1)}) custom-call(bf16[4,128,256]{2,1,0:T(8,128)(2,1)} %bitcast.81, bf16[128,2048]{1,0:T(8,128)(2,1)} %get-tuple-element.49.refs_1_), custom_call_target="tpu_custom_call" | custom-call | tf_op jit(solution)/shard_map/pallas_call | solution.py:190
  55.7 1.6 reduce_sum.78.chunk_ref
  57.3 24.1 %shard_map.113 = (bf16[4,128,256]{2,1,0:T(8,128)(2,1)}, bf16[4,128,2048]{2,1,0:T(8,128)(2,1)}) custom-call(bf16[128,256]{1,0:T(8,128)(2,1)} %reduce_sum.78.chunk_ref, bf16[128,2048]{1,0:T(8,128)(2,1)} %get-tuple-element.48.extra_ref), custom_call_target="tpu_custom_call" | custom-call | tf_op jit(solution)/shard_map/pallas_call | solution.py:190
  81.4 1.1 copy.13
  82.5 2.8 pad_maximum_fusion
  85.3 2.3 multiply_reduce_fusion.1
  88.4 42.1 %shard_map.114 = (bf16[4,1,128,2048]{3,2,1,0:T(8,128)(2,1)}, bf16[4,128,2048]{2,1,0:T(8,128)(2,1)}, f32[4,8,128]{2,1,0:T(8,128)}) custom-call(bf16[128,2048]{1,0:T(8,128)(2,1)} %get-tuple-element.47.own_ref, f32[8,128]{1,0:T(8,128)} %broadcast_in_dim.14.sum_ref), custom_call_target="tpu_custom_call" | custom-call | tf_op jit(solution)/shard_map/pallas_call | solution.py:190
  130.5 10.0 %convolution_convert_fusion = bf16[512,2048]{1,0:T(8,128)(2,1)} fusion(bf16[512,2048]{1,0:T(8,128)(2,1)} %bitcast.85, bf16[1,2048,2048]{2,1,0:T(8,128)(2,1)} %param.11), kind=kOutput, calls=%fused_computation.2 | convolution fusion | flops 4296015872 | bytes 12582912 | tf_op jit(solution)/shard_map/dot_general | solution.py:701
  140.5 1.4 convolution_convert_fusion.3
  141.9 1.4 convolution_convert_fusion.2
  143.3 42.2 %shard_map.115 = (bf16[4,128,2048]{2,1,0:T(8,128)(2,1)}, bf16[4,128,256]{2,1,0:T(8,128)(2,1)}, bf16[4,128,256]{2,1,0:T(8,128)(2,1)}) custom-call(bf16[4,128,2048]{2,1,0:T(8,128)(2,1)} %bitcast.71, bf16[4,128,256]{2,1,0:T(8,128)(2,1)} %bitcast.78, bf16[4,128,256]{2,1,0:T(8,128)(2,1)} %bitcast.79), custom_call_target="tpu_custom_call" | custom-call | tf_op jit(solution)/shard_map/pallas_call | solution.py:190
  187.2 1.6 copy-done.1
  190.7 10.7 %shard_map.116 = (bf16[128,2048]{1,0:T(8,128)(2,1)}, bf16[128,2048]{1,0:T(8,128)(2,1)S(1)}, bf16[128,256]{1,0:T(8,128)(2,1)S(1)}, bf16[128,256]{1,0:T(8,128)(2,1)S(1)}) custom-call(bf16[4,128,2048]{2,1,0:T(8,128)(2,1)S(1)} %copy-done.1, bf16[4,128,256]{2,1,0:T(8,128)(2,1)S(1)} %copy-done.6, bf16[4,128,256]{2,1,0:T(8,128)(2,1)S(1)} %copy-done.7, ...), custom_call_target="tpu_custom_call" | custom-call | tf_op jit(solution)/shard_map/pallas_call | solution.py:610
  201.4 3.4 copy-done
  204.8 94.7 %shard_map.117 = (bf16[4,128,2048]{2,1,0:T(8,128)(2,1)S(1)}, bf16[4,128,256]{2,1,0:T(8,128)(2,1)S(1)}) custom-call(bf16[128,2048]{1,0:T(8,128)(2,1)S(1)} %get-tuple-element.36.refs_0_, bf16[128,256]{1,0:T(8,128)(2,1)S(1)} %get-tuple-element.37.refs_1_, bf16[128,256]{1,0:T(8,128)(2,1)S(1)} %get-tuple-element.38.refs_2_, bf16[2048,2048]{1,0:T(8,128)(2,1)S(1)} %bitcast.62, ...), custom_call_target="tpu_custom_call" | custom-call | tf_op jit(solution)/shard_map/pallas_call | solution.py:535
  301.5 17.7 %shard_map.118 = f32[4,8,128]{2,1,0:T(8,128)} custom-call(f32[8,128]{1,0:T(8,128)} %broadcast_in_dim.17.refs_0_), custom_call_target="tpu_custom_call" | custom-call | tf_op jit(solution)/shard_map/pallas_call | solution.py:190
  320.2 4.7 %convolution_convert_fusion.5 = bf16[128,1024]{1,0:T(8,128)(2,1)} fusion(bf16[128,2048]{1,0:T(8,128)(2,1)S(1)} %subtract_convert_fusion.refs_1_, bf16[1024,2048]{1,0:T(8,128)(2,1)} %bitcast.68), kind=kOutput, calls=%fused_computation.10 | convolution fusion | flops 537001984 | bytes 4980736 | tf_op jit(solution)/shard_map/dot_general | solution.py:689
  324.9 23.5 %shard_map.119 = (bf16[4,32,1024]{2,1,0:T(8,128)(2,1)}, bf16[4,128,2048]{2,1,0:T(8,128)(2,1)}) custom-call(bf16[4,32,1024]{2,1,0:T(8,128)(2,1)} %bitcast.72, bf16[128,2048]{1,0:T(8,128)(2,1)} %copy-done.12), custom_call_target="tpu_custom_call" | custom-call | tf_op jit(solution)/shard_map/pallas_call | solution.py:190
  350.1 13.1 %shard_map.120 = (bf16[4,32,1024]{2,1,0:T(8,128)(2,1)}, bf16[4,4,32,256]{3,2,1,0:T(8,128)(2,1)}) custom-call(bf16[32,1024]{1,0:T(8,128)(2,1)} %copy-done.16, bf16[4,32,256]{2,1,0:T(8,128)(2,1)} %bitcast.82), custom_call_target="tpu_custom_call" | custom-call | tf_op jit(solution)/shard_map/pallas_call | solution.py:190
  363.2 3.1 convolution_bitcast_fusion.1
  366.4 2.0 convolution_bitcast_fusion
  368.4 3.7 fusion
  (59 shorter events, 10.9 us)
Async XLA Ops:
  7.2 22.3 %copy-start.14 = (bf16[1,256,2048]{2,1,0:T(8,128)(2,1)S(1)}, bf16[1,256,2048]{2,1,0:T(8,128)(2,1)}, u32[]{:S(2)}) copy-start(bf16[1,256,2048]{2,1,0:T(8,128)(2,1)} %param.10) | copy-start | bytes 3145732
  7.2 361.3 %all-gather.2.cloned.1.call-start = ((), (), s32[]{:S(2)}) async-start(), calls=%async_computation | async-start | bytes 5242880 | tf_op jit(solution)/shard_map/all_gather | solution.py:758
  7.2 23.3 %copy-start.15 = (bf16[1,256,2048]{2,1,0:T(8,128)(2,1)S(1)}, bf16[1,256,2048]{2,1,0:T(8,128)(2,1)}, u32[]{:S(2)}) copy-start(bf16[1,256,2048]{2,1,0:T(8,128)(2,1)} %param.9) | copy-start | bytes 3145732
  29.5 2.0 copy-start.10
  85.3 2.4 copy-start.8
  130.5 10.0 %copy-start.3 = (bf16[1,2048,256]{2,1,0:T(8,128)(2,1)S(1)}, bf16[1,2048,256]{2,1,0:T(8,128)(2,1)}, u32[]{:S(2)}) copy-start(bf16[1,2048,256]{2,1,0:T(8,128)(2,1)} %param.12) | copy-start | bytes 3145732
  130.5 10.0 %copy-start.19 = (bf16[4,1,128,2048]{3,2,1,0:T(8,128)(2,1)S(1)}, bf16[4,1,128,2048]{3,2,1,0:T(8,128)(2,1)}, u32[]{:S(2)}) copy-start(bf16[4,1,128,2048]{3,2,1,0:T(8,128)(2,1)} %get-tuple-element.29) | copy-start | bytes 6291460
  140.5 1.4 copy-start.4
  143.3 43.1 %copy-start.18 = (s32[1,1,128]{2,1,0:T(1,128)S(1)}, s32[1,1,128]{2,1,0:T(1,128)}, u32[]{:S(2)}) copy-start(s32[1,1,128]{2,1,0:T(1,128)} %param.14) | copy-start | bytes 1540
  143.3 43.9 %copy-start.5 = (bf16[1,128,2048]{2,1,0:T(8,128)(2,1)S(1)}, bf16[1,128,2048]{2,1,0:T(8,128)(2,1)}, u32[]{:S(2)}) copy-start(bf16[1,128,2048]{2,1,0:T(8,128)(2,1)} %param.15) | copy-start | bytes 1572868
  185.6 15.8 %copy-start.2 = (bf16[4,128,256]{2,1,0:T(8,128)(2,1)S(1)}, bf16[4,128,256]{2,1,0:T(8,128)(2,1)}, u32[]{:S(2)}) copy-start(bf16[4,128,256]{2,1,0:T(8,128)(2,1)} %get-tuple-element.26.refs_6_) | copy-start | bytes 786436
  187.2 1.6 copy-start.1
  188.8 0.9 copy-start.6
  189.7 1.0 copy-start.7
  201.4 3.4 copy-start
  299.5 1.2 copy-start.9
  320.2 4.7 %copy-start.12 = (bf16[128,2048]{1,0:T(8,128)(2,1)}, bf16[128,2048]{1,0:T(8,128)(2,1)S(1)}, u32[]{:S(2)}) copy-start(bf16[128,2048]{1,0:T(8,128)(2,1)S(1)} %subtract_convert_fusion.refs_1_) | copy-start | bytes 1572868
  320.2 43.0 %copy-start.11 = (bf16[4,128,2048]{2,1,0:T(8,128)(2,1)S(1)}, bf16[4,128,2048]{2,1,0:T(8,128)(2,1)}, u32[]{:S(2)}) copy-start(bf16[4,128,2048]{2,1,0:T(8,128)(2,1)} %shard_map.111) | copy-start | bytes 6291460
  349.4 0.7 copy-start.16
  363.2 3.2 copy-start.13
  366.4 2.1 copy-start.17
Sparse Core Ops, SparseCore 0:
  185.7 81.3 all-gather.1

commit v4 on v3

--- a/solution.py
+++ b/solution.py
@@ -754,8 +754,6 @@
         (dot(columns, wk).astype(low).reshape(rows, tokens, key_width), "fsdp", "scatter"),
         (dot(columns, wv).astype(low).reshape(rows, tokens, key_width), "fsdp", "scatter"),
     )
-    query_parts, encoder = lax.optimization_barrier((query_parts, encoder))
-    encoder_rows = lax.all_gather(encoder, "fsdp", axis=0, tiled=True)
     mixed, query_grad, key_grad, value_grad = attend(
         query_parts, key_parts, value_parts, norm_factor, out_grad[0], segments[0, 0]
     )
@@ -765,9 +763,12 @@
     )
     whole = rows * tokens
     normed_grad = summed(grad_parts)
-    (inner_parts,) = exchange(
-        9, (as_rows(jnp.sum(normed_grad * decoded, axis=1)), "tensor", "gather")
-    )
+    inner_parts, encoder_rows = exchange(
+        9,
+        (as_rows(jnp.sum(normed_grad * decoded, axis=1)), "tensor", "gather"),
+        (encoder, "fsdp", "gather"),
+    )
+    encoder_rows = encoder_rows.reshape(rows * code_rows, width)
     inner_dot = jnp.sum(inner_parts[:, 0], axis=0)[:, None]
     decoded_grad = (norm_factor * normed_grad - decoded * norm_factor**3 * inner_dot / D).astype(
         low

time: 380 us -> 390 us (1.026)
  Pallas kernels: 313 us -> 331 us
  between operations: 14.3 us -> 0.9 us
    pallas_call x8, Pallas kernels: 208 us -> 240 us  [any_call(): pl.pallas_call(kernel, out_shape=shapes, in_specs=[pl.BlockSpec(memory_sp...]
    pallas_call x1, Pallas kernels: 94.7 us -> 80.3 us  [back_to_features(): pl.pallas_call(back_kernel, out_shape=[jax.ShapeDtypeStruct((cols, tokens...]
    unnamed x40 -> x32, local copies, waits for them, and re-layouts: 8.8 us -> 7.76 us
  transfers between devices with their start and end apart: 1 -> 0, of which waited for: 0 -> 0; matrix products, arithmetic and copies ran while one was open for 4% -> 0% of each run, Pallas kernels for 42% -> 0%
where the time goes in v4:
time: 390 us; the launch traced here: 389 us
  Pallas kernels  331 us (85%)
  matrix products  33.4 us (9%)
  local copies, waits for them, and re-layouts  12.2 us (3%)
  other arithmetic  12 us (3%)
    pallas_call x8, Pallas kernels, any_call(): pl.pallas_call(kernel, out_shape=shapes, in_specs=[pl.BlockSpec(memory_sp...  240 us
    pallas_call x1, Pallas kernels, back_to_features(): pl.pallas_call(back_kernel, out_shape=[jax.ShapeDtypeStruct((cols, tokens...  80.3 us
    dot_general x5, matrix products, dot(): return jnp.dot(left, right, preferred_element_type=jnp.float32)  21.6 us
    pallas_call x1, Pallas kernels, attend(): pl.pallas_call(functools.partial(attend_kernel, wide // DH), grid=(pair_c...  10.7 us

profile of v4, /device:TPU:0, one launch (start us, length us, event | category | flops | bytes accessed | tf_op | source)
XLA Modules:
  0.0 389.2 jit_solution(8888987434103899258)
XLA Ops:
  2.8 2.4 slice_bitcast_fusion
  5.2 22.2 %shard_map.111 = bf16[4,128,2048]{2,1,0:T(8,128)(2,1)} custom-call(bf16[128,2048]{1,0:T(8,128)(2,1)} %bitcast.78), custom_call_target="tpu_custom_call" | custom-call | tf_op jit(solution)/shard_map/pallas_call | solution.py:190
  27.4 3.0 convolution_convert_fusion.4
  30.4 22.8 %shard_map.112 = (bf16[4,128,256]{2,1,0:T(8,128)(2,1)}, bf16[4,128,2048]{2,1,0:T(8,128)(2,1)}) custom-call(bf16[4,128,256]{2,1,0:T(8,128)(2,1)} %bitcast.83, bf16[128,2048]{1,0:T(8,128)(2,1)} %get-tuple-element.49.refs_1_), custom_call_target="tpu_custom_call" | custom-call | tf_op jit(solution)/shard_map/pallas_call | solution.py:190
  53.2 1.6 reduce_sum.78.chunk_ref
  54.8 24.1 %shard_map.113 = (bf16[4,128,256]{2,1,0:T(8,128)(2,1)}, bf16[4,128,2048]{2,1,0:T(8,128)(2,1)}) custom-call(bf16[128,256]{1,0:T(8,128)(2,1)} %reduce_sum.78.chunk_ref, bf16[128,2048]{1,0:T(8,128)(2,1)} %get-tuple-element.48.extra_ref), custom_call_target="tpu_custom_call" | custom-call | tf_op jit(solution)/shard_map/pallas_call | solution.py:190
  78.9 4.8 %pad_maximum_fusion = bf16[4,256,2048]{2,1,0:T(8,128)(2,1)} fusion(bf16[4,128,2048]{2,1,0:T(8,128)(2,1)} %get-tuple-element.28, bf16[4,128,2048]{2,1,0:T(8,128)(2,1)} %get-tuple-element.27), kind=kLoop, calls=%fused_computation | loop fusion | flops 8388608 | bytes 8388608 | tf_op jit(solution)/shard_map/concatenate | solution.py:740
  83.9 4.2 %multiply_reduce_fusion.1 = (f32[128]{0:T(128)S(1)}, bf16[128,2048]{1,0:T(8,128)(2,1)}, f32[128,2048]{1,0:T(8,128)}) fusion(bf16[128,1024]{0,1:T(8,128)(2,1)S(1)} %bitcast.75, bf16[1024,2048]{1,0:T(8,128)(2,1)} %bitcast.68), kind=kOutput, calls=%fused_computation.13 | convolution fusion | flops 537657216 | bytes 6029824 | tf_op jit(solution)/shard_map/dot_general | solution.py:701
  88.7 42.1 %shard_map.114 = (bf16[4,1,128,2048]{3,2,1,0:T(8,128)(2,1)}, bf16[4,128,2048]{2,1,0:T(8,128)(2,1)}, f32[4,8,128]{2,1,0:T(8,128)}) custom-call(bf16[128,2048]{1,0:T(8,128)(2,1)} %get-tuple-element.47.own_ref, f32[8,128]{1,0:T(8,128)} %broadcast_in_dim.14.sum_ref), custom_call_target="tpu_custom_call" | custom-call | tf_op jit(solution)/shard_map/pallas_call | solution.py:190
  131.8 3.0 convolution_convert_fusion.2
  134.8 1.4 convolution_convert_fusion.3
  136.2 9.1 %convolution_convert_fusion = bf16[512,2048]{1,0:T(8,128)(2,1)} fusion(bf16[512,2048]{1,0:T(8,128)(2,1)S(1)} %bitcast.89, bf16[1,2048,2048]{2,1,0:T(8,128)(2,1)} %param.11), kind=kOutput, calls=%fused_computation.2 | convolution fusion | flops 4296015872 | bytes 12582912 | tf_op jit(solution)/shard_map/dot_general | solution.py:701
  145.3 42.2 %shard_map.115 = (bf16[4,128,2048]{2,1,0:T(8,128)(2,1)}, bf16[4,128,256]{2,1,0:T(8,128)(2,1)}, bf16[4,128,256]{2,1,0:T(8,128)(2,1)}) custom-call(bf16[4,128,2048]{2,1,0:T(8,128)(2,1)} %bitcast.73, bf16[4,128,256]{2,1,0:T(8,128)(2,1)} %bitcast.81, bf16[4,128,256]{2,1,0:T(8,128)(2,1)} %bitcast.80), custom_call_target="tpu_custom_call" | custom-call | tf_op jit(solution)/shard_map/pallas_call | solution.py:190
  187.6 1.6 copy-done.1
  191.1 10.7 %shard_map.116 = (bf16[128,2048]{1,0:T(8,128)(2,1)}, bf16[128,2048]{1,0:T(8,128)(2,1)S(1)}, bf16[128,256]{1,0:T(8,128)(2,1)S(1)}, bf16[128,256]{1,0:T(8,128)(2,1)S(1)}) custom-call(bf16[4,128,2048]{2,1,0:T(8,128)(2,1)S(1)} %copy-done.1, bf16[4,128,256]{2,1,0:T(8,128)(2,1)S(1)} %copy-done.6, bf16[4,128,256]{2,1,0:T(8,128)(2,1)S(1)} %copy-done.7, ...), custom_call_target="tpu_custom_call" | custom-call | tf_op jit(solution)/shard_map/pallas_call | solution.py:610
  201.7 3.4 copy-done
  205.1 80.3 %shard_map.117 = (bf16[4,128,2048]{2,1,0:T(8,128)(2,1)S(1)}, bf16[4,128,256]{2,1,0:T(8,128)(2,1)S(1)}) custom-call(bf16[128,2048]{1,0:T(8,128)(2,1)S(1)} %get-tuple-element.35.refs_0_, bf16[128,256]{1,0:T(8,128)(2,1)S(1)} %get-tuple-element.36.refs_1_, bf16[128,256]{1,0:T(8,128)(2,1)S(1)} %get-tuple-element.37.refs_2_, bf16[2048,2048]{1,0:T(8,128)(2,1)S(1)} %bitcast.63, ...), custom_call_target="tpu_custom_call" | custom-call | tf_op jit(solution)/shard_map/pallas_call | solution.py:535
  287.4 51.5 %shard_map.118 = (f32[4,8,128]{2,1,0:T(8,128)}, bf16[4,256,2048]{2,1,0:T(8,128)(2,1)}) custom-call(f32[8,128]{1,0:T(8,128)} %broadcast_in_dim.17.refs_0_, bf16[256,2048]{1,0:T(8,128)(2,1)} %bitcast.76), custom_call_target="tpu_custom_call" | custom-call | tf_op jit(solution)/shard_map/pallas_call | solution.py:190
  340.0 4.6 %convolution_convert_fusion.5 = bf16[128,1024]{1,0:T(8,128)(2,1)} fusion(bf16[128,2048]{1,0:T(8,128)(2,1)S(1)} %subtract_convert_fusion.refs_1_, bf16[1024,2048]{1,0:T(8,128)(2,1)} %bitcast.69), kind=kOutput, calls=%fused_computation.10 | convolution fusion | flops 537001984 | bytes 4980736 | tf_op jit(solution)/shard_map/dot_general | solution.py:689
  344.6 21.7 %shard_map.119 = (bf16[4,32,1024]{2,1,0:T(8,128)(2,1)}, bf16[4,128,2048]{2,1,0:T(8,128)(2,1)}) custom-call(bf16[4,32,1024]{2,1,0:T(8,128)(2,1)} %bitcast.74, bf16[128,2048]{1,0:T(8,128)(2,1)} %copy-done.10), custom_call_target="tpu_custom_call" | custom-call | tf_op jit(solution)/shard_map/pallas_call | solution.py:190
  368.0 13.1 %shard_map.120 = (bf16[4,32,1024]{2,1,0:T(8,128)(2,1)}, bf16[4,4,32,256]{3,2,1,0:T(8,128)(2,1)}) custom-call(bf16[32,1024]{1,0:T(8,128)(2,1)} %copy-done.13, bf16[4,32,256]{2,1,0:T(8,128)(2,1)} %bitcast.84), custom_call_target="tpu_custom_call" | custom-call | tf_op jit(solution)/shard_map/pallas_call | solution.py:190
  381.2 3.9 %fusion = bf16[1,128,2048]{2,1,0:T(8,128)(2,1)} fusion(bf16[128,1024]{1,0:T(8,128)(2,1)} %bitcast.82, bf16[1024,2048]{1,0:T(8,128)(2,1)} %bitcast.72), kind=kOutput, calls=%fused_computation.6 | convolution fusion | flops 537133056 | bytes 4980736 | tf_op jit(solution)/shard_map/dot_general | solution.py:701
  385.1 2.1 convolution_bitcast_fusion.1
  387.2 2.1 convolution_bitcast_fusion
  (48 shorter events, 10.5 us)
Async XLA Ops:
  2.8 24.5 %copy-start.12 = (bf16[1,256,2048]{2,1,0:T(8,128)(2,1)S(1)}, bf16[1,256,2048]{2,1,0:T(8,128)(2,1)}, u32[]{:S(2)}) copy-start(bf16[1,256,2048]{2,1,0:T(8,128)(2,1)} %param.9) | copy-start | bytes 3145732
  78.9 4.8 %copy-start.2 = (bf16[4,128,256]{2,1,0:T(8,128)(2,1)S(1)}, bf16[4,128,256]{2,1,0:T(8,128)(2,1)}, u32[]{:S(2)}) copy-start(bf16[4,128,256]{2,1,0:T(8,128)(2,1)} %get-tuple-element.26.refs_6_) | copy-start | bytes 786436
  83.9 47.9 %copy-start.4 = (bf16[1,2048,256]{2,1,0:T(8,128)(2,1)S(1)}, bf16[1,2048,256]{2,1,0:T(8,128)(2,1)}, u32[]{:S(2)}) copy-start(bf16[1,2048,256]{2,1,0:T(8,128)(2,1)} %param.13) | copy-start | bytes 3145732
  130.8 4.0 %copy-start.3 = (bf16[1,2048,256]{2,1,0:T(8,128)(2,1)S(1)}, bf16[1,2048,256]{2,1,0:T(8,128)(2,1)}, u32[]{:S(2)}) copy-start(bf16[1,2048,256]{2,1,0:T(8,128)(2,1)} %param.12) | copy-start | bytes 3145732
  130.8 4.0 %copy-start.15 = (bf16[4,1,128,2048]{3,2,1,0:T(8,128)(2,1)S(1)}, bf16[4,1,128,2048]{3,2,1,0:T(8,128)(2,1)}, u32[]{:S(2)}) copy-start(bf16[4,1,128,2048]{3,2,1,0:T(8,128)(2,1)} %get-tuple-element.29) | copy-start | bytes 6291460
  145.3 42.2 %copy-start.5 = (bf16[1,128,2048]{2,1,0:T(8,128)(2,1)S(1)}, bf16[1,128,2048]{2,1,0:T(8,128)(2,1)}, u32[]{:S(2)}) copy-start(bf16[1,128,2048]{2,1,0:T(8,128)(2,1)} %param.15) | copy-start | bytes 1572868
  187.6 1.6 copy-start.1
  189.2 0.9 copy-start.6
  190.1 0.9 copy-start.7
  201.7 3.4 copy-start
  285.4 1.2 copy-start.8
  340.0 4.6 %copy-start.10 = (bf16[128,2048]{1,0:T(8,128)(2,1)}, bf16[128,2048]{1,0:T(8,128)(2,1)S(1)}, u32[]{:S(2)}) copy-start(bf16[128,2048]{1,0:T(8,128)(2,1)S(1)} %subtract_convert_fusion.refs_1_) | copy-start | bytes 1572868
  367.3 0.7 copy-start.13
  381.1 4.0 %copy-start.9 = (bf16[4,128,2048]{2,1,0:T(8,128)(2,1)S(1)}, bf16[4,128,2048]{2,1,0:T(8,128)(2,1)}, u32[]{:S(2)}) copy-start(bf16[4,128,2048]{2,1,0:T(8,128)(2,1)} %shard_map.111) | copy-start | bytes 6291460
  381.1 3.9 %copy-start.14 = (bf16[4,4,32,256]{3,2,1,0:T(8,128)(2,1)S(1)}, bf16[4,4,32,256]{3,2,1,0:T(8,128)(2,1)}, u32[]{:S(2)}) copy-start(bf16[4,4,32,256]{3,2,1,0:T(8,128)(2,1)} %get-tuple-element.43) | copy-start | bytes 786436
  385.1 2.1 copy-start.11
